TPU v7x, 32 devices: a whole 2x2x4 slice. The times are simulated.
32 devices in a mesh: dp: 16 (over z, x, core), tensor: 2 (over y).
Axes of the slice: x: 2, y: 2, z: 4, core: 2. Of those that a mesh axis runs over, the one named last changes fastest.
Arguments:
- tokens: bfloat16 [16384, 1536], P('dp'), may hold values from -6 to 6
- cotangent: bfloat16 [16384, 1536], P('dp'), may hold values from -6 to 6
- segments: int32 [32, 256], P('dp'), may hold values from 0 to 3, never falling along the last dimension, each value on 1 to 128 neighbouring positions
- gain_attn: float32 [1536], replicated, may hold values from 0.5 to 1.5
- w_query: bfloat16 [1536, 1536], P(None, 'tensor'), may hold values from -0.15625 to 0.15625
- w_key: bfloat16 [1536, 1536], P(None, 'tensor'), may hold values from -0.15625 to 0.15625
- w_value: bfloat16 [1536, 1536], P(None, 'tensor'), may hold values from -0.15625 to 0.15625
- w_outgate: bfloat16 [1536, 1536], P(None, 'tensor'), may hold values from -0.15625 to 0.15625
- w_forget: bfloat16 [1536, 24], P(None, 'tensor'), may hold values from -0.15625 to 0.15625
- b_forget: float32 [24], P('tensor'), may hold values from 2 to 7
- w_out: bfloat16 [1536, 1536], P('tensor'), may hold values from -0.4375 to 0.4375
- gain_mlp: float32 [1536], replicated, may hold values from 0.5 to 1.5
- w_gate: bfloat16 [1536, 4096], P(None, 'tensor'), may hold values from -0.15625 to 0.15625
- w_up: bfloat16 [1536, 4096], P(None, 'tensor'), may hold values from -0.15625 to 0.15625
- w_down: bfloat16 [4096, 1536], P('tensor'), may hold values from -0.09375 to 0.09375
Outputs:
- result: bfloat16 [16384, 1536], P('dp')
- d_tokens: bfloat16 [16384, 1536], P('dp')
- g_gain_attn: float32 [1536], P('dp')
- g_query: float32 [1536, 1536], P('dp', 'tensor')
- g_key: float32 [1536, 1536], P('dp', 'tensor')
- g_value: float32 [1536, 1536], P('dp', 'tensor')
- g_outgate: float32 [1536, 1536], P('dp', 'tensor')
- g_forget: float32 [1536, 24], P('dp', 'tensor')
- g_forget_bias: float32 [24], P('tensor')
- g_out: float32 [1536, 1536], P('tensor', 'dp')
- g_gain_mlp: float32 [1536], P('dp')
- g_gate: float32 [1536, 4096], P('dp', 'tensor')
- g_up: float32 [1536, 4096], P('dp', 'tensor')
- g_down: float32 [4096, 1536], P('tensor', 'dp')
Inputs may be any that keep to these rules, and one draw needn't show every extreme that they name: `segments`: in each row the continuation numbers never fall; each of the 4 continuations has 1 to 128 rows, and one has exactly 128.
All inputs are finite; a program needn't handle non-finite values.
Results may differ from a plain program's by a relative error of at most 0.025.
Values may be sent and summed in bfloat16 or wider, within the bound.
No kernel may reach another device: no remote copies, remote signals or barrier semaphores. Data moves between devices by JAX's collectives and lax.ppermute only.
A program may use at most 384 MiB of HBM per device.

v0:
```python
import jax
import jax.numpy as jnp
from jax import lax
from jax.sharding import PartitionSpec as P

MICRO = 2
PROMPT = 256
CONT_TOK = 256


EPS = 1e-06


def matmul_f32(first_arg, second_arg):
    return jnp.dot(first_arg, second_arg, preferred_element_type=jnp.float32)


def contract_rows(first_arg, second_arg):
    return lax.dot_general(
        first_arg, second_arg, (((0,), (0,)), ((), ())), preferred_element_type=jnp.float32
    )


def contract_cols(first_arg, second_arg):
    return lax.dot_general(
        first_arg, second_arg, (((1,), (1,)), ((), ())), preferred_element_type=jnp.float32
    )


def rms_forward(values, gain):
    row_scale = lax.rsqrt(jnp.mean(values * values, axis=-1, keepdims=True) + EPS)
    return (values * row_scale * gain, row_scale)


def rms_backward(values, row_scale, gain, d_norm):
    weighted = d_norm * gain
    inner_mean = jnp.mean(weighted * values, axis=-1, keepdims=True)
    d_values = row_scale * weighted - values * (row_scale * row_scale * row_scale) * inner_mean
    d_gain = jnp.sum(d_norm * values * row_scale, axis=0)
    return (d_values, d_gain)


def path_mask(segment_row):
    ident = jnp.concatenate([jnp.full((PROMPT,), -1, jnp.int32), segment_row])
    total_rows = ident.shape[0]
    row_ids = lax.broadcasted_iota(jnp.int32, (total_rows, total_rows), 0)
    col_ids = lax.broadcasted_iota(jnp.int32, (total_rows, total_rows), 1)
    same_path = jnp.logical_or(ident[None, :] == -1, ident[None, :] == ident[:, None])
    return jnp.logical_and(col_ids <= row_ids, same_path)


def masked_scores(queries, keys_low, decay_sum, allowed, head_scale):
    raw = (
        jnp.einsum("qhd,khd->hqk", queries, keys_low, preferred_element_type=jnp.float32)
        * head_scale
    )
    raw = raw + decay_sum.T[:, :, None] - decay_sum.T[:, None, :]
    return jnp.where(allowed[None], raw, -1e30)


def micro_step(x_rows, d_rows, segment_row, params):
    (
        gain_attn,
        w_query,
        w_key,
        w_value,
        w_outgate,
        w_forget,
        b_forget,
        w_out,
        gain_mlp,
        w_gate,
        w_up,
        w_down,
    ) = params
    row_count = x_rows.shape[0]
    share_rows = row_count // lax.axis_size("tensor")
    share_start = lax.axis_index("tensor") * share_rows
    head_count = w_forget.shape[1]
    head_size = w_query.shape[1] // head_count
    head_scale = head_size ** (-0.5)
    x_full = x_rows.astype(jnp.float32)
    normed_attn, scale_attn = rms_forward(x_full, gain_attn)
    act_attn = normed_attn.astype(jnp.bfloat16)
    x_share = lax.dynamic_slice_in_dim(x_full, share_start, share_rows, 0)
    scale_attn_share = lax.dynamic_slice_in_dim(scale_attn, share_start, share_rows, 0)
    queries = (
        matmul_f32(act_attn, w_query).astype(jnp.bfloat16).reshape(row_count, head_count, head_size)
    )
    keys_low = (
        matmul_f32(act_attn, w_key).astype(jnp.bfloat16).reshape(row_count, head_count, head_size)
    )
    values_low = (
        matmul_f32(act_attn, w_value).astype(jnp.bfloat16).reshape(row_count, head_count, head_size)
    )
    gate_pre = matmul_f32(act_attn, w_outgate)
    forget_pre = matmul_f32(act_attn, w_forget) + b_forget
    log_forget = jax.nn.log_sigmoid(forget_pre)
    allowed = path_mask(segment_row)
    ancestry = allowed.astype(jnp.float32)
    decay_sum = jnp.dot(ancestry, log_forget, precision=lax.Precision.HIGHEST)
    scores = masked_scores(queries, keys_low, decay_sum, allowed, head_scale)
    row_max = jnp.max(scores, axis=-1, keepdims=True)
    exp_scores = jnp.exp(scores - row_max)
    row_total = jnp.sum(exp_scores, axis=-1, keepdims=True)
    log_total = row_max + jnp.log(row_total)
    probs_low = (exp_scores / row_total).astype(jnp.bfloat16)
    attended = jnp.einsum(
        "hqk,khd->qhd", probs_low, values_low, preferred_element_type=jnp.float32
    ).reshape(row_count, head_count * head_size)
    gate_value = jax.nn.sigmoid(gate_pre)
    gated = (attended * gate_value).astype(jnp.bfloat16)
    attn_share = lax.psum_scatter(
        matmul_f32(gated, w_out).astype(jnp.bfloat16), "tensor", scatter_dimension=0, tiled=True
    ).astype(jnp.float32)
    hidden = x_share + attn_share
    normed_mlp, scale_mlp = rms_forward(hidden, gain_mlp)
    act_share = normed_mlp.astype(jnp.bfloat16)
    act_mlp = lax.all_gather(act_share, "tensor", axis=0, tiled=True)
    gate_mlp = matmul_f32(act_mlp, w_gate)
    up_mlp = matmul_f32(act_mlp, w_up)
    gate_sigmoid = jax.nn.sigmoid(gate_mlp)
    silu_value = gate_mlp * gate_sigmoid
    inner_act = (silu_value * up_mlp).astype(jnp.bfloat16)
    mlp_share = lax.psum_scatter(
        matmul_f32(inner_act, w_down).astype(jnp.bfloat16),
        "tensor",
        scatter_dimension=0,
        tiled=True,
    ).astype(jnp.float32)
    result_share = (hidden + mlp_share).astype(jnp.bfloat16)
    d_result = lax.dynamic_slice_in_dim(d_rows, share_start, share_rows, 0).astype(jnp.float32)
    g_down = contract_rows(inner_act, d_rows)
    d_inner = contract_cols(d_rows, w_down)
    d_gate_mlp = (d_inner * up_mlp * gate_sigmoid * (1.0 + gate_mlp * (1.0 - gate_sigmoid))).astype(
        jnp.bfloat16
    )
    d_up_mlp = (d_inner * silu_value).astype(jnp.bfloat16)
    g_gate = contract_rows(act_mlp, d_gate_mlp)
    g_up = contract_rows(act_mlp, d_up_mlp)
    d_act_mlp = lax.psum_scatter(
        (contract_cols(d_gate_mlp, w_gate) + contract_cols(d_up_mlp, w_up)).astype(jnp.bfloat16),
        "tensor",
        scatter_dimension=0,
        tiled=True,
    ).astype(jnp.float32)
    d_norm_mlp, g_gain_mlp = rms_backward(hidden, scale_mlp, gain_mlp, d_act_mlp)
    d_hidden = d_result + d_norm_mlp
    d_attn = lax.all_gather(d_hidden.astype(jnp.bfloat16), "tensor", axis=0, tiled=True)
    g_out = contract_rows(gated, d_attn)
    d_gated = contract_cols(d_attn, w_out)
    d_attended = (
        (d_gated * gate_value).astype(jnp.bfloat16).reshape(row_count, head_count, head_size)
    )
    d_gate_pre = (d_gated * attended * gate_value * (1.0 - gate_value)).astype(jnp.bfloat16)
    d_probs = jnp.einsum("qhd,khd->hqk", d_attended, values_low, preferred_element_type=jnp.float32)
    d_values = (
        jnp.einsum("hqk,qhd->khd", probs_low, d_attended, preferred_element_type=jnp.float32)
        .astype(jnp.bfloat16)
        .reshape(row_count, head_count * head_size)
    )
    probs_again = jnp.exp(
        masked_scores(queries, keys_low, decay_sum, allowed, head_scale) - log_total
    )
    row_inner = jnp.sum(probs_again * d_probs, axis=-1, keepdims=True)
    d_scores = (probs_again * (d_probs - row_inner)).astype(jnp.bfloat16)
    d_queries = (
        (
            jnp.einsum("hqk,khd->qhd", d_scores, keys_low, preferred_element_type=jnp.float32)
            * head_scale
        )
        .astype(jnp.bfloat16)
        .reshape(row_count, head_count * head_size)
    )
    d_keys = (
        (
            jnp.einsum("hqk,qhd->khd", d_scores, queries, preferred_element_type=jnp.float32)
            * head_scale
        )
        .astype(jnp.bfloat16)
        .reshape(row_count, head_count * head_size)
    )
    d_decay = (
        jnp.sum(d_scores, axis=2, dtype=jnp.float32) - jnp.sum(d_scores, axis=1, dtype=jnp.float32)
    ).T
    d_log_forget = jnp.dot(ancestry.T, d_decay, precision=lax.Precision.HIGHEST)
    d_forget_pre = (d_log_forget * jax.nn.sigmoid(-forget_pre)).astype(jnp.bfloat16)
    g_query = contract_rows(act_attn, d_queries)
    g_key = contract_rows(act_attn, d_keys)
    g_value = contract_rows(act_attn, d_values)
    g_outgate = contract_rows(act_attn, d_gate_pre)
    g_forget = contract_rows(act_attn, d_forget_pre)
    g_bias = jnp.sum(d_forget_pre, axis=0, dtype=jnp.float32)
    d_act_part = (
        contract_cols(d_queries, w_query)
        + contract_cols(d_keys, w_key)
        + contract_cols(d_values, w_value)
    )
    d_act_part = (
        d_act_part + contract_cols(d_gate_pre, w_outgate) + contract_cols(d_forget_pre, w_forget)
    )
    d_act_attn = lax.psum_scatter(
        d_act_part.astype(jnp.bfloat16), "tensor", scatter_dimension=0, tiled=True
    ).astype(jnp.float32)
    d_norm_attn, g_gain_attn = rms_backward(x_share, scale_attn_share, gain_attn, d_act_attn)
    d_input_share = (d_hidden + d_norm_attn).astype(jnp.bfloat16)
    result, d_input = (
        lax.all_gather(result_share, "tensor", axis=0, tiled=True),
        lax.all_gather(d_input_share, "tensor", axis=0, tiled=True),
    )
    gradients = (
        g_gain_attn,
        g_query,
        g_key,
        g_value,
        g_outgate,
        g_forget,
        g_bias,
        g_out,
        g_gain_mlp,
        g_gate,
        g_up,
        g_down,
    )
    return (result, d_input, gradients)


def local(
    tokens,
    cotangent,
    segments,
    gain_attn,
    w_query,
    w_key,
    w_value,
    w_outgate,
    w_forget,
    b_forget,
    w_out,
    gain_mlp,
    w_gate,
    w_up,
    w_down,
):
    params = (
        gain_attn,
        w_query,
        w_key,
        w_value,
        w_outgate,
        w_forget,
        b_forget,
        w_out,
        gain_mlp,
        w_gate,
        w_up,
        w_down,
    )
    group_rows = PROMPT + CONT_TOK
    dp_devices = lax.axis_size("dp")
    empty_outputs = (jnp.zeros(tokens.shape, jnp.bfloat16), jnp.zeros(tokens.shape, jnp.bfloat16))

    def run_micro(micro_index, outputs):
        row_start = micro_index * group_rows
        x_rows = lax.dynamic_slice_in_dim(tokens, row_start, group_rows, 0)
        d_rows = lax.dynamic_slice_in_dim(cotangent, row_start, group_rows, 0)
        segment_row = lax.dynamic_slice_in_dim(segments, micro_index, 1, 0)[0]
        result, d_input, gradients = micro_step(x_rows, d_rows, segment_row, params)
        result_all = lax.dynamic_update_slice_in_dim(outputs[0], result, row_start, 0)
        d_tokens_all = lax.dynamic_update_slice_in_dim(outputs[1], d_input, row_start, 0)
        return ((result_all, d_tokens_all), gradients)

    def step_end(micro_index, loop_state):
        outputs, totals = loop_state
        outputs, gradients = run_micro(micro_index, outputs)
        return (
            outputs,
            tuple((first_arg + second_arg for first_arg, second_arg in zip(totals, gradients))),
        )

    zero_grads = tuple((jnp.zeros(weight.shape, jnp.float32) for weight in params))
    outputs, totals = lax.fori_loop(0, MICRO, step_end, (empty_outputs, zero_grads))
    (
        t_gain_attn,
        t_query,
        t_key,
        t_value,
        t_outgate,
        t_forget,
        t_bias,
        t_out,
        t_gain_mlp,
        t_gate,
        t_up,
        t_down,
    ) = totals
    row_shares = (
        lax.psum_scatter(t_query, "dp", scatter_dimension=0, tiled=True),
        lax.psum_scatter(t_key, "dp", scatter_dimension=0, tiled=True),
        lax.psum_scatter(t_value, "dp", scatter_dimension=0, tiled=True),
        lax.psum_scatter(t_outgate, "dp", scatter_dimension=0, tiled=True),
        lax.psum_scatter(t_forget, "dp", scatter_dimension=0, tiled=True),
        lax.psum_scatter(t_gate, "dp", scatter_dimension=0, tiled=True),
        lax.psum_scatter(t_up, "dp", scatter_dimension=0, tiled=True),
    )
    col_shares = (
        lax.psum_scatter(t_out, "dp", scatter_dimension=1, tiled=True),
        lax.psum_scatter(t_down, "dp", scatter_dimension=1, tiled=True),
    )
    gain_local = (t_gain_attn, t_gain_mlp)
    gain_attn_total, gain_mlp_total = lax.psum((gain_local[0], gain_local[1]), ("dp", "tensor"))
    gain_rows = gain_attn.shape[0] // dp_devices
    gain_start = lax.axis_index("dp") * gain_rows
    s_gain_attn = lax.dynamic_slice_in_dim(gain_attn_total, gain_start, gain_rows, 0)
    s_gain_mlp = lax.dynamic_slice_in_dim(gain_mlp_total, gain_start, gain_rows, 0)
    bias_total = lax.psum(t_bias, "dp")
    s_query, s_key, s_value, s_outgate, s_forget, s_gate, s_up = row_shares
    s_out, s_down = col_shares
    return (
        outputs[0],
        outputs[1],
        s_gain_attn,
        s_query,
        s_key,
        s_value,
        s_outgate,
        s_forget,
        bias_total,
        s_out,
        s_gain_mlp,
        s_gate,
        s_up,
        s_down,
    )


def solution(mesh):
    in_specs = (
        P("dp", None),
        P("dp", None),
        P("dp", None),
        P(),
        P(None, "tensor"),
        P(None, "tensor"),
        P(None, "tensor"),
        P(None, "tensor"),
        P(None, "tensor"),
        P("tensor"),
        P("tensor", None),
        P(),
        P(None, "tensor"),
        P(None, "tensor"),
        P("tensor", None),
    )
    out_specs = (
        P("dp", None),
        P("dp", None),
        P("dp"),
        P("dp", "tensor"),
        P("dp", "tensor"),
        P("dp", "tensor"),
        P("dp", "tensor"),
        P("dp", "tensor"),
        P("tensor"),
        P("tensor", "dp"),
        P("dp"),
        P("dp", "tensor"),
        P("dp", "tensor"),
        P("tensor", "dp"),
    )
    return jax.shard_map(local, mesh=mesh, in_specs=in_specs, out_specs=out_specs, check_vma=False)
```

profile of v0, /device:TPU:0, one launch (start us, length us, event | category | flops | bytes accessed | tf_op | source)
XLA Modules:
  0.0 1623.2 jit_solution(1864004422368192485)
XLA Ops:
  11.9 732.5 %while.40 = (s32[]{:T(128)}, bf16[1024,1536]{1,0:T(8,128)(2,1)}, bf16[1024,1536]{1,0:T(8,128)(2,1)}, f32[1536]{0:T(1024)}, f32[1536,768]{1,0:T(8,128)}, /*index=...) while((s32[]{:T(128)}, bf16[1024,1536]{1,0:T(8,128)(2,1)}, ...), condition=%wide.region_17.18_spmd.clone, body=%wide.region_0.17_spmd.clone.sunk | while | flops 49839849472 | bytes 866261504 | solution.py:282
  26.5 5.4 fusion.235
  45.3 5.4 fusion.237
  53.7 5.0 multiply_convert_fusion.46
  64.3 26.8 %reduce-scatter.34.cloned.1.call-done = bf16[256,1536]{1,0:T(8,128)(2,1)} async-done(((bf16[512,1536]{1,0:T(8,128)(2,1)}), bf16[256,1536]{1,0:T(8,128)(2,1)}) %reduce-scatter.34.cloned.1.call-update) | async-done | bytes 786448 | tf_op jit(solution)/shard_map/while/body/eval_jaxpr/reduce_scatter | solution.py:113
  94.4 27.3 %all-gather.5.cloned.1.call-done = bf16[512,1536]{1,0:T(8,128)(2,1)} async-done(((bf16[256,1536]{1,0:T(8,128)(2,1)}), bf16[512,1536]{1,0:T(8,128)(2,1)}) %all-gather.5.cloned.1.call-update) | async-done | bytes 1572880 | tf_op jit(solution)/shard_map/while/body/eval_jaxpr/all_gather | solution.py:119
  121.7 6.9 fusion.238
  128.6 8.1 fusion.239
  136.7 9.4 multiply_convert_fusion.48
  146.1 7.3 fusion.240
  153.4 7.6 fusion.241
  161.1 26.2 %reduce-scatter.36.cloned.1.call-done = bf16[256,1536]{1,0:T(8,128)(2,1)} async-done(((bf16[512,1536]{1,0:T(8,128)(2,1)}), bf16[256,1536]{1,0:T(8,128)(2,1)}) %reduce-scatter.36.cloned.1.call-update) | async-done | bytes 786448 | tf_op jit(solution)/shard_map/while/body/eval_jaxpr/reduce_scatter | solution.py:141
  191.9 27.3 %all-gather.7.cloned.1.call-done = bf16[512,1536]{1,0:T(8,128)(2,1)} async-done(((bf16[256,1536]{1,0:T(8,128)(2,1)}), bf16[512,1536]{1,0:T(8,128)(2,1)}) %all-gather.7.cloned.1.call-update) | async-done | bytes 1572880 | tf_op jit(solution)/shard_map/while/body/eval_jaxpr/all_gather | solution.py:149
  219.2 5.3 multiply_convert_fusion.49
  226.0 11.0 multiply_reduce_fusion.8
  238.8 7.0 convert_reduce_fusion.5
  260.2 7.7 convolution_convert_fusion.17
  268.0 8.0 select_add_fusion.29
  276.0 6.5 select_add_fusion.27
  282.5 6.7 select_add_fusion.28
  291.5 23.2 %reduce-scatter.40.cloned.1.call-done = bf16[256,1536]{1,0:T(8,128)(2,1)} async-done(((bf16[512,1536]{1,0:T(8,128)(2,1)}), bf16[256,1536]{1,0:T(8,128)(2,1)}) %reduce-scatter.40.cloned.1.call-update) | async-done | bytes 786448 | tf_op jit(solution)/shard_map/while/body/eval_jaxpr/reduce_scatter | solution.py:125
  314.6 4.2 fusion.247
  321.3 5.0 select_add_fusion.23
  333.9 5.0 select_add_fusion.24
  348.9 26.7 %all-gather.9.cloned.1.call-done = bf16[512,1536]{1,0:T(8,128)(2,1)} async-done(((bf16[256,1536]{1,0:T(8,128)(2,1)}), bf16[512,1536]{1,0:T(8,128)(2,1)}) %all-gather.9.cloned.1.call-update) | async-done | bytes 1572880 | tf_op jit(solution)/shard_map/while/body/eval_jaxpr/all_gather | solution.py:208
  392.7 5.0 fusion.235
  411.1 5.4 fusion.237
  419.5 5.0 multiply_convert_fusion.46
  430.1 24.1 %reduce-scatter.34.cloned.1.call-done = bf16[256,1536]{1,0:T(8,128)(2,1)} async-done(((bf16[512,1536]{1,0:T(8,128)(2,1)}), bf16[256,1536]{1,0:T(8,128)(2,1)}) %reduce-scatter.34.cloned.1.call-update) | async-done | bytes 786448 | tf_op jit(solution)/shard_map/while/body/eval_jaxpr/reduce_scatter | solution.py:113
  457.5 27.3 %all-gather.5.cloned.1.call-done = bf16[512,1536]{1,0:T(8,128)(2,1)} async-done(((bf16[256,1536]{1,0:T(8,128)(2,1)}), bf16[512,1536]{1,0:T(8,128)(2,1)}) %all-gather.5.cloned.1.call-update) | async-done | bytes 1572880 | tf_op jit(solution)/shard_map/while/body/eval_jaxpr/all_gather | solution.py:119
  484.9 7.2 fusion.238
  492.1 8.1 fusion.239
  500.2 9.4 multiply_convert_fusion.48
  509.5 7.3 fusion.240
  516.9 7.6 fusion.241
  524.6 26.2 %reduce-scatter.36.cloned.1.call-done = bf16[256,1536]{1,0:T(8,128)(2,1)} async-done(((bf16[512,1536]{1,0:T(8,128)(2,1)}), bf16[256,1536]{1,0:T(8,128)(2,1)}) %reduce-scatter.36.cloned.1.call-update) | async-done | bytes 786448 | tf_op jit(solution)/shard_map/while/body/eval_jaxpr/reduce_scatter | solution.py:141
  555.4 27.3 %all-gather.7.cloned.1.call-done = bf16[512,1536]{1,0:T(8,128)(2,1)} async-done(((bf16[256,1536]{1,0:T(8,128)(2,1)}), bf16[512,1536]{1,0:T(8,128)(2,1)}) %all-gather.7.cloned.1.call-update) | async-done | bytes 1572880 | tf_op jit(solution)/shard_map/while/body/eval_jaxpr/all_gather | solution.py:149
  582.7 5.3 multiply_convert_fusion.49
  589.4 10.9 multiply_reduce_fusion.8
  602.3 7.0 convert_reduce_fusion.5
  623.7 7.5 convolution_convert_fusion.17
  631.2 9.7 select_add_fusion.29
  641.0 9.5 select_add_fusion.27
  650.5 9.7 select_add_fusion.28
  662.4 15.7 reduce-scatter.40.cloned.1.call-done
  678.1 4.2 fusion.247
  684.8 6.4 select_add_fusion.23
  691.3 6.2 select_add_fusion.22
  697.5 6.2 select_add_fusion.21
  703.7 6.4 select_add_fusion.24
  710.1 6.0 select_add_fusion.25
  718.8 20.2 %all-gather.9.cloned.1.call-done = bf16[512,1536]{1,0:T(8,128)(2,1)} async-done(((bf16[256,1536]{1,0:T(8,128)(2,1)}), bf16[512,1536]{1,0:T(8,128)(2,1)}) %all-gather.9.cloned.1.call-update) | async-done | bytes 1572880 | tf_op jit(solution)/shard_map/while/body/eval_jaxpr/all_gather | solution.py:208
  746.6 6.0 copy.67
  755.5 12.8 copy.68
  769.7 33.9 %psum.22 = f32[12]{0:T(128)} all-reduce(f32[12]{0:T(128)S(1)} %copy-done.46), channel_id=1, replica_groups=mesh['dp'=16,'tensor'=2] {'dp'}, use_global_device_ids=true, to_apply=%region_24.25 | all-reduce | flops 12 | bytes 96 | tf_op jit(solution)/shard_map/psum | solution.py:316
  803.5 37.0 %all-reduce.1 = (f32[1536]{0:T(1024)S(1)}, f32[1536]{0:T(1024)S(1)}) all-reduce(f32[1536]{0:T(1024)S(1)} %copy-done.38, f32[1536]{0:T(1024)S(1)} %copy-done.41), channel_id=1, replica_groups=mesh['dp'=16,'tensor'=2] {'dp','tensor'}, use_global_device_ids=true, to_apply=%region_18.19 | all-reduce | flops 3072 | bytes 24576 | tf_op jit(solution)/shard_map/psum | solution.py:311
  843.2 41.3 %reduce-scatter.24.cloned.1.call-done = f32[768,96]{0,1:T(8,128)} async-done(((f32[768,1536]{0,1:T(8,128)}), f32[768,96]{0,1:T(8,128)}) %reduce-scatter.24.cloned.1.call-update) | async-done | bytes 294928 | tf_op jit(solution)/shard_map/reduce_scatter | solution.py:307
  884.5 78.7 %reduce-scatter.16.cloned.1.call-done = f32[96,768]{1,0:T(8,128)} async-done(((f32[1536,768]{1,0:T(8,128)}), f32[96,768]{1,0:T(8,128)}) %reduce-scatter.16.cloned.1.call-update) | async-done | bytes 294928 | tf_op jit(solution)/shard_map/reduce_scatter | solution.py:298
  963.2 79.4 %reduce-scatter.18.cloned.1.call-done = f32[96,768]{1,0:T(8,128)} async-done(((f32[1536,768]{1,0:T(8,128)}), f32[96,768]{1,0:T(8,128)}) %reduce-scatter.18.cloned.1.call-update) | async-done | bytes 294928 | tf_op jit(solution)/shard_map/reduce_scatter | solution.py:299
  1042.6 78.8 %reduce-scatter.20.cloned.1.call-done = f32[96,768]{1,0:T(8,128)} async-done(((f32[1536,768]{1,0:T(8,128)}), f32[96,768]{1,0:T(8,128)}) %reduce-scatter.20.cloned.1.call-update) | async-done | bytes 294928 | tf_op jit(solution)/shard_map/reduce_scatter | solution.py:300
  1121.4 79.3 %reduce-scatter.22.cloned.1.call-done = f32[96,768]{1,0:T(8,128)} async-done(((f32[1536,768]{1,0:T(8,128)}), f32[96,768]{1,0:T(8,128)}) %reduce-scatter.22.cloned.1.call-update) | async-done | bytes 294928 | tf_op jit(solution)/shard_map/reduce_scatter | solution.py:301
  1200.7 138.1 %reduce-scatter.30.cloned.1.call-done = f32[2048,96]{0,1:T(8,128)} async-done(((f32[2048,1536]{0,1:T(8,128)}), f32[2048,96]{0,1:T(8,128)}) %reduce-scatter.30.cloned.1.call-update) | async-done | bytes 786448 | tf_op jit(solution)/shard_map/reduce_scatter | solution.py:308
  1338.9 138.3 %reduce-scatter.26.cloned.1.call-done = f32[96,2048]{1,0:T(8,128)} async-done(((f32[1536,2048]{1,0:T(8,128)}), f32[96,2048]{1,0:T(8,128)}) %reduce-scatter.26.cloned.1.call-update) | async-done | bytes 786448 | tf_op jit(solution)/shard_map/reduce_scatter | solution.py:303
  1477.2 138.3 %reduce-scatter.28.cloned.1.call-done = f32[96,2048]{1,0:T(8,128)} async-done(((f32[1536,2048]{1,0:T(8,128)}), f32[96,2048]{1,0:T(8,128)}) %reduce-scatter.28.cloned.1.call-update) | async-done | bytes 786448 | tf_op jit(solution)/shard_map/reduce_scatter | solution.py:304
  (384 shorter events, 171.1 us)
Async XLA Ops:
  12.3 78.8 %reduce-scatter.34.cloned.1.call-start = ((), (), s32[]{:S(2)}) async-start(), calls=%async_computation.22 | async-start | bytes 2359296 | tf_op jit(solution)/shard_map/while/body/eval_jaxpr/reduce_scatter | solution.py:113
  62.1 59.6 %all-gather.5.cloned.1.call-start = ((), (), s32[]{:S(2)}) async-start(), calls=%async_computation.23 | async-start | bytes 2359296 | tf_op jit(solution)/shard_map/while/body/eval_jaxpr/all_gather | solution.py:119
  93.0 95.9 %copy-start.1 = (f32[256,1536]{1,0:T(8,128)}, f32[256,1536]{1,0:T(8,128)S(1)}, u32[]{:S(2)}) copy-start(f32[256,1536]{1,0:T(8,128)S(1)} %get-tuple-element.902) | copy-start | bytes 4718596 | tf_op jit(solution)/shard_map/while
  94.3 93.0 %reduce-scatter.36.cloned.1.call-start = ((), (), s32[]{:S(2)}) async-start(), calls=%async_computation.24 | async-start | bytes 2359296 | tf_op jit(solution)/shard_map/while/body/eval_jaxpr/reduce_scatter | solution.py:141
  128.6 8.1 copy-start.19
  146.1 7.3 copy-start.27
  146.1 7.3 copy-start.25
  161.1 58.2 %all-gather.7.cloned.1.call-start = ((), (), s32[]{:S(2)}) async-start(), calls=%async_computation.25 | async-start | bytes 2359296 | tf_op jit(solution)/shard_map/while/body/eval_jaxpr/all_gather | solution.py:149
  161.1 58.1 %copy-start.31 = (f32[512,768]{1,0:T(8,128)S(1)}, f32[512,768]{1,0:T(8,128)}, u32[]{:S(2)}) copy-start(f32[512,768]{1,0:T(8,128)} %copy.83) | copy-start | bytes 4718596 | tf_op jit(solution)/shard_map/while
  191.9 97.4 %reduce-scatter.38.cloned.1.call-start = ((), (), s32[]{:S(2)}) async-start(), calls=%async_computation.26 | async-start | bytes 2359296 | tf_op jit(solution)/shard_map/while/body/eval_jaxpr/reduce_scatter | solution.py:202
  225.9 11.0 copy-start.11
  225.9 11.0 slice-start
  226.0 11.0 slice-start.1
  226.0 12.9 slice-start.2
  226.0 23.0 %slice-start.3 = ((s8[6291456]{0:T(1024)(128)(4,1)}), s8[4194304]{0:T(1024)(128)(4,1)S(1)}, s32[]{:S(2)}) async-start(s8[6291456]{0:T(1024)(128)(4,1)} %bitcast.206), calls=%async_computation.33 | async-start | bytes 8388608 | tf_op jit(solution)/shard_map/while
  238.8 10.2 slice-start.4
  260.1 54.5 %reduce-scatter.40.cloned.1.call-start = ((), (), s32[]{:S(2)}) async-start(), calls=%async_computation.27 | async-start | bytes 2359296 | tf_op jit(solution)/shard_map/while/body/eval_jaxpr/reduce_scatter | solution.py:125
  267.9 78.4 %all-gather.11.cloned.1.call-start = ((), (), s32[]{:S(2)}) async-start(), calls=%async_computation.29 | async-start | bytes 2359296 | tf_op jit(solution)/shard_map/while/body/eval_jaxpr/all_gather | solution.py:209
  268.0 8.0 copy-start.7
  268.0 8.0 copy-start.28
  282.5 32.1 %copy-start.13 = (bf16[256,1536]{1,0:T(8,128)(2,1)S(1)}, bf16[256,1536]{1,0:T(8,128)(2,1)}, u32[]{:S(2)}) copy-start(bf16[256,1536]{1,0:T(8,128)(2,1)} %reduce-scatter.36.cloned.1.call-done) | copy-start | bytes 2359300 | tf_op jit(solution)/shard_map/while
  289.2 25.4 %copy-start.2 = (f32[256,1536]{1,0:T(8,128)S(1)}, f32[256,1536]{1,0:T(8,128)}, u32[]{:S(2)}) copy-start(f32[256,1536]{1,0:T(8,128)} %copy-done.1) | copy-start | bytes 4718596 | tf_op jit(solution)/shard_map/while
  289.2 29.7 %copy-start.40 = (f32[1536]{0:T(1024)}, f32[1536]{0:T(1024)S(1)}, u32[]{:S(2)}) copy-start(f32[1536]{0:T(1024)S(1)} %select_add_fusion.26) | copy-start | bytes 18436 | tf_op jit(solution)/shard_map/while
  318.9 56.7 %all-gather.9.cloned.1.call-start = ((), (), s32[]{:S(2)}) async-start(), calls=%async_computation.28 | async-start | bytes 2359296 | tf_op jit(solution)/shard_map/while/body/eval_jaxpr/all_gather | solution.py:208
  342.6 35.7 %copy-start.37 = (f32[1536]{0:T(1024)}, f32[1536]{0:T(1024)S(1)}, u32[]{:S(2)}) copy-start(f32[1536]{0:T(1024)S(1)} %select_add_fusion.20) | copy-start | bytes 18436 | tf_op jit(solution)/shard_map/while
  346.3 32.0 %copy-start.51 = (f32[12]{0:T(128)S(1)}, f32[12]{0:T(128)}, u32[]{:S(2)}) copy-start(f32[12]{0:T(128)} %get-tuple-element.1175) | copy-start | bytes 148 | tf_op jit(solution)/shard_map/while
  378.5 75.7 %reduce-scatter.34.cloned.1.call-start = ((), (), s32[]{:S(2)}) async-start(), calls=%async_computation.22 | async-start | bytes 2359296 | tf_op jit(solution)/shard_map/while/body/eval_jaxpr/reduce_scatter | solution.py:113
  428.0 56.9 %all-gather.5.cloned.1.call-start = ((), (), s32[]{:S(2)}) async-start(), calls=%async_computation.23 | async-start | bytes 2359296 | tf_op jit(solution)/shard_map/while/body/eval_jaxpr/all_gather | solution.py:119
  456.2 96.2 %copy-start.1 = (f32[256,1536]{1,0:T(8,128)}, f32[256,1536]{1,0:T(8,128)S(1)}, u32[]{:S(2)}) copy-start(f32[256,1536]{1,0:T(8,128)S(1)} %get-tuple-element.902) | copy-start | bytes 4718596 | tf_op jit(solution)/shard_map/while
  457.5 93.3 %reduce-scatter.36.cloned.1.call-start = ((), (), s32[]{:S(2)}) async-start(), calls=%async_computation.24 | async-start | bytes 2359296 | tf_op jit(solution)/shard_map/while/body/eval_jaxpr/reduce_scatter | solution.py:141
  492.1 8.1 copy-start.19
  509.5 7.3 copy-start.25
  524.5 58.2 %all-gather.7.cloned.1.call-start = ((), (), s32[]{:S(2)}) async-start(), calls=%async_computation.25 | async-start | bytes 2359296 | tf_op jit(solution)/shard_map/while/body/eval_jaxpr/all_gather | solution.py:149
  524.6 58.1 %copy-start.31 = (f32[512,768]{1,0:T(8,128)S(1)}, f32[512,768]{1,0:T(8,128)}, u32[]{:S(2)}) copy-start(f32[512,768]{1,0:T(8,128)} %copy.83) | copy-start | bytes 4718596 | tf_op jit(solution)/shard_map/while
  555.3 104.9 %reduce-scatter.38.cloned.1.call-start = ((), (), s32[]{:S(2)}) async-start(), calls=%async_computation.26 | async-start | bytes 2359296 | tf_op jit(solution)/shard_map/while/body/eval_jaxpr/reduce_scatter | solution.py:202
  589.4 11.0 copy-start.11
  589.4 11.0 slice-start
  589.4 11.1 slice-start.1
  589.4 12.9 slice-start.2
  589.4 23.0 %slice-start.3 = ((s8[6291456]{0:T(1024)(128)(4,1)}), s8[4194304]{0:T(1024)(128)(4,1)S(1)}, s32[]{:S(2)}) async-start(s8[6291456]{0:T(1024)(128)(4,1)} %bitcast.206), calls=%async_computation.33 | async-start | bytes 8388608 | tf_op jit(solution)/shard_map/while
  602.3 10.2 slice-start.4
  623.5 54.6 %reduce-scatter.40.cloned.1.call-start = ((), (), s32[]{:S(2)}) async-start(), calls=%async_computation.27 | async-start | bytes 2359296 | tf_op jit(solution)/shard_map/while/body/eval_jaxpr/reduce_scatter | solution.py:125
  631.2 84.9 %all-gather.11.cloned.1.call-start = ((), (), s32[]{:S(2)}) async-start(), calls=%async_computation.29 | async-start | bytes 2359296 | tf_op jit(solution)/shard_map/while/body/eval_jaxpr/all_gather | solution.py:209
  631.2 9.8 copy-start.7
  631.2 9.7 copy-start.28
  641.0 9.5 copy-start.26
  650.5 9.7 copy-start.39
  650.5 27.6 %copy-start.13 = (bf16[256,1536]{1,0:T(8,128)(2,1)S(1)}, bf16[256,1536]{1,0:T(8,128)(2,1)}, u32[]{:S(2)}) copy-start(bf16[256,1536]{1,0:T(8,128)(2,1)} %reduce-scatter.36.cloned.1.call-done) | copy-start | bytes 2359300 | tf_op jit(solution)/shard_map/while
  660.1 18.0 %copy-start.2 = (f32[256,1536]{1,0:T(8,128)S(1)}, f32[256,1536]{1,0:T(8,128)}, u32[]{:S(2)}) copy-start(f32[256,1536]{1,0:T(8,128)} %copy-done.1) | copy-start | bytes 4718596 | tf_op jit(solution)/shard_map/while
  660.1 22.2 %copy-start.40 = (f32[1536]{0:T(1024)}, f32[1536]{0:T(1024)S(1)}, u32[]{:S(2)}) copy-start(f32[1536]{0:T(1024)S(1)} %select_add_fusion.26) | copy-start | bytes 18436 | tf_op jit(solution)/shard_map/while
  682.4 56.6 %all-gather.9.cloned.1.call-start = ((), (), s32[]{:S(2)}) async-start(), calls=%async_computation.28 | async-start | bytes 2359296 | tf_op jit(solution)/shard_map/while/body/eval_jaxpr/all_gather | solution.py:208
  716.1 25.5 %copy-start.37 = (f32[1536]{0:T(1024)}, f32[1536]{0:T(1024)S(1)}, u32[]{:S(2)}) copy-start(f32[1536]{0:T(1024)S(1)} %select_add_fusion.20) | copy-start | bytes 18436 | tf_op jit(solution)/shard_map/while
  716.1 25.5 %copy-start.51 = (f32[12]{0:T(128)S(1)}, f32[12]{0:T(128)}, u32[]{:S(2)}) copy-start(f32[12]{0:T(128)} %get-tuple-element.1175) | copy-start | bytes 148 | tf_op jit(solution)/shard_map/while
  744.4 97.3 %reduce-scatter.32.cloned.1.call-start = ((), (), s32[]{:S(2)}) async-start(), calls=%async_computation.21 | async-start | bytes 835584
  746.5 137.9 %reduce-scatter.24.cloned.1.call-start = ((), (), s32[]{:S(2)}) async-start(), calls=%async_computation.17 | async-start | bytes 5013504 | tf_op jit(solution)/shard_map/reduce_scatter | solution.py:307
  752.7 210.5 %reduce-scatter.16.cloned.1.call-start = ((), (), s32[]{:S(2)}) async-start(), calls=%async_computation.13 | async-start | bytes 5013504 | tf_op jit(solution)/shard_map/reduce_scatter | solution.py:298
  753.2 289.3 %reduce-scatter.18.cloned.1.call-start = ((), (), s32[]{:S(2)}) async-start(), calls=%async_computation.14 | async-start | bytes 5013504 | tf_op jit(solution)/shard_map/reduce_scatter | solution.py:299
  754.0 367.4 %reduce-scatter.20.cloned.1.call-start = ((), (), s32[]{:S(2)}) async-start(), calls=%async_computation.15 | async-start | bytes 5013504 | tf_op jit(solution)/shard_map/reduce_scatter | solution.py:300
  754.7 446.0 %reduce-scatter.22.cloned.1.call-start = ((), (), s32[]{:S(2)}) async-start(), calls=%async_computation.16 | async-start | bytes 5013504 | tf_op jit(solution)/shard_map/reduce_scatter | solution.py:301
  755.5 583.4 %reduce-scatter.30.cloned.1.call-start = ((), (), s32[]{:S(2)}) async-start(), calls=%async_computation.20 | async-start | bytes 13369344 | tf_op jit(solution)/shard_map/reduce_scatter | solution.py:308
  768.4 708.8 %reduce-scatter.26.cloned.1.call-start = ((), (), s32[]{:S(2)}) async-start(), calls=%async_computation.18 | async-start | bytes 13369344 | tf_op jit(solution)/shard_map/reduce_scatter | solution.py:303
  768.9 846.6 %reduce-scatter.28.cloned.1.call-start = ((), (), s32[]{:S(2)}) async-start(), calls=%async_computation.19 | async-start | bytes 13369344 | tf_op jit(solution)/shard_map/reduce_scatter | solution.py:304
  769.0 34.5 %copy-start.38 = (f32[1536]{0:T(1024)S(1)}, f32[1536]{0:T(1024)}, u32[]{:S(2)}) copy-start(f32[1536]{0:T(1024)} %get-tuple-element.1140) | copy-start | bytes 18436
  769.0 34.5 %copy-start.41 = (f32[1536]{0:T(1024)S(1)}, f32[1536]{0:T(1024)}, u32[]{:S(2)}) copy-start(f32[1536]{0:T(1024)} %get-tuple-element.1148) | copy-start | bytes 18436
  (67 other events, 272.5 us)
Sparse Core Ops, SparseCore 0:
  62.3 28.7 reduce-scatter.33
  94.5 27.1 all-gather.4
  161.2 26.0 reduce-scatter.35
  192.0 27.1 all-gather.6
  260.2 26.1 reduce-scatter.37
  288.5 26.0 reduce-scatter.39
  319.0 27.2 all-gather.10
  348.4 27.2 all-gather.8
  428.1 26.0 reduce-scatter.33
  457.6 27.2 all-gather.4
  524.6 26.0 reduce-scatter.35
  555.4 27.2 all-gather.6
  623.7 26.0 reduce-scatter.37
  652.0 26.0 reduce-scatter.39
  682.5 27.2 all-gather.10
  711.7 27.1 all-gather.8
Sparse Core Ops, SparseCore 1:
  748.4 56.6 reduce-scatter.31
  809.9 74.5 reduce-scatter.23
  888.8 74.4 reduce-scatter.15
  968.1 74.4 reduce-scatter.17
  1047.0 74.3 reduce-scatter.19
  1126.3 74.3 reduce-scatter.21
  1205.2 133.6 reduce-scatter.29
  1343.4 133.8 reduce-scatter.25
  1481.7 133.8 reduce-scatter.27
where the time goes:
time: 1630 us; the launch traced here: 1620 us
  waiting for transfers between devices  1080 us (66%)
  matrix products  317 us (19%)
  local copies, waits for them, and re-layouts  75.3 us (5%)
  blocking collectives  70.8 us (4%)
  other arithmetic  59.7 us (4%)
    reduce_scatter x1, waiting for transfers between devices, local(): lax.psum_scatter(t_up, 'dp', scatter_dimension=0, tiled=True)  138 us
    reduce_scatter x1, waiting for transfers between devices, local(): lax.psum_scatter(t_gate, 'dp', scatter_dimension=0, tiled=True)  138 us
    reduce_scatter x1, waiting for transfers between devices, local(): lax.psum_scatter(t_down, 'dp', scatter_dimension=1, tiled=True)  138 us
    dot_general x18, matrix products, contract_rows(): lax.dot_general(first_arg, second_arg, (((0,), (0,)), ((), ())), preferre...  107 us
    reduce_scatter x1, waiting for transfers between devices, local(): lax.psum_scatter(t_key, 'dp', scatter_dimension=0, tiled=True)  79.4 us
    reduce_scatter x1, waiting for transfers between devices, local(): lax.psum_scatter(t_outgate, 'dp', scatter_dimension=0, tiled=True)  79.3 us
    dot_general x18, matrix products, matmul_f32(): return jnp.dot(first_arg, second_arg, preferred_element_type=jnp.float32)  79 us
    reduce_scatter x1, waiting for transfers between devices, local(): lax.psum_scatter(t_value, 'dp', scatter_dimension=0, tiled=True)  78.8 us
  transfers between devices with their start and end apart: 25, of which 21 were waited for; matrix products, arithmetic and copies ran while one was open for 10% of the time, Pallas kernels for 0%

commit v1 on v0

v1 whole, which is shorter than its diff:
```python
import functools

import jax
import jax.numpy as jnp
from jax import lax
from jax.experimental import pallas as pl
from jax.experimental.pallas import tpu as pltpu
from jax.sharding import PartitionSpec as P

PROMPT = 256
CONT_TOK = 256
GROUP = PROMPT + CONT_TOK
LANES = 128
HEAD = 64
BLOCK_HEADS = 4
BLOCK_COLS = HEAD * BLOCK_HEADS
EPS = 1e-06
NEG = -1e30
BF = jnp.bfloat16
F32 = jnp.float32


def dot_dims(first_arg, second_arg, first_dim, second_dim):
    return lax.dot_general(
        first_arg,
        second_arg,
        (((first_dim,), (second_dim,)), ((), ())),
        preferred_element_type=F32,
    )


def dot_nn(first_arg, second_arg):
    return dot_dims(first_arg, second_arg, 1, 0)


def dot_nt(first_arg, second_arg):
    return dot_dims(first_arg, second_arg, 1, 1)


def dot_tn(first_arg, second_arg):
    return dot_dims(first_arg, second_arg, 0, 0)


def sigmoid(values):
    return 1.0 / (1.0 + jnp.exp(-values))


def split_three(values):
    high = values.astype(BF).astype(F32)
    rest = values - high
    middle = rest.astype(BF).astype(F32)
    return high, middle, rest - middle


def visible_pairs(ident_row_ref, ident_col_ref):
    row_ids = lax.broadcasted_iota(jnp.int32, (GROUP, GROUP), 0)
    col_ids = lax.broadcasted_iota(jnp.int32, (GROUP, GROUP), 1)
    ident_row = ident_row_ref[...]
    same = jnp.logical_or(ident_row == -1, ident_row == ident_col_ref[...])
    return jnp.logical_and(col_ids <= row_ids, same)


def lane_ids():
    return lax.broadcasted_iota(jnp.int32, (GROUP, LANES), 1)


def place_extras(lanes, own, main, base, extras, constant_at):
    value = jnp.where(
        jnp.logical_and(lanes >= base + constant_at, lanes < base + constant_at + 3), 1.0, 0.0
    )
    offset = 0 if constant_at else 3
    for position, column in enumerate(extras):
        value = jnp.where(lanes == base + offset + position, column, value)
    return jnp.where(own, main, value).astype(BF)


def column_of(lanes, values, index):
    return jnp.sum(jnp.where(lanes == index, values, 0.0), axis=1, keepdims=True)


def attn_fwd_kernel(
    x_ref,
    ident_row_ref,
    ident_col_ref,
    gain_ref,
    wq_ref,
    wk_ref,
    wv_ref,
    wg_ref,
    wf_ref,
    bias_ref,
    wo_ref,
    part_ref,
    act_ref,
    q_ref,
    k_ref,
    v_ref,
    sig_ref,
    att_ref,
    gated_ref,
    lse_ref,
    decay_ref,
    forget_ref,
    acc_ref,
    mask_ref,
):
    step = pl.program_id(0)
    lanes = lane_ids()

    @pl.when(step == 0)
    def _():
        x = x_ref[...].astype(F32)
        scale = lax.rsqrt(jnp.mean(x * x, axis=1, keepdims=True) + EPS)
        act = (x * scale * gain_ref[...]).astype(BF)
        act_ref[...] = act
        forget_pre = dot_nn(act, wf_ref[...]) + bias_ref[...]
        forget_ref[...] = forget_pre
        log_forget = jnp.minimum(forget_pre, 0.0) - jnp.log1p(jnp.exp(-jnp.abs(forget_pre)))
        allowed = visible_pairs(ident_row_ref, ident_col_ref)
        mask_ref[...] = jnp.where(allowed, 0.0, NEG)
        ancestry = jnp.where(allowed, 1.0, 0.0).astype(BF)
        high, middle, low = split_three(log_forget)
        decay_ref[...] = (
            dot_nn(ancestry, high.astype(BF))
            + dot_nn(ancestry, middle.astype(BF))
            + dot_nn(ancestry, low.astype(BF))
        )
        acc_ref[...] = jnp.zeros_like(acc_ref)
        lse_ref[...] = jnp.zeros_like(lse_ref)

    act = act_ref[...]
    queries = dot_nn(act, wq_ref[...]).astype(BF)
    keys_low = dot_nn(act, wk_ref[...]).astype(BF)
    values_low = dot_nn(act, wv_ref[...]).astype(BF)
    gate = sigmoid(dot_nn(act, wg_ref[...]))
    q_ref[...] = queries
    k_ref[...] = keys_low
    v_ref[...] = values_low
    sig_ref[...] = gate
    attended_pairs = []
    for pair in range(BLOCK_HEADS // 2):
        cols = slice(pair * LANES, (pair + 1) * LANES)
        q_pair = queries[:, cols].astype(F32) * (HEAD**-0.5)
        k_pair = keys_low[:, cols].astype(F32)
        v_pair = values_low[:, cols]
        outs = []
        for half in range(2):
            own = (lanes < HEAD) if half == 0 else (lanes >= HEAD)
            base = HEAD if half == 0 else 0
            head = step * BLOCK_HEADS + pair * 2 + half
            decay = column_of(lanes, decay_ref[...], head)
            parts = split_three(decay)
            q_ext = place_extras(lanes, own, q_pair, base, parts, 3)
            k_ext = place_extras(lanes, own, k_pair, base, [-value for value in parts], 0)
            scores_p = dot_nt(q_ext[:PROMPT], k_ext[:PROMPT]) + mask_ref[:PROMPT, :PROMPT]
            scores_a = dot_nt(q_ext[PROMPT:], k_ext[:PROMPT])
            scores_b = dot_nt(q_ext[PROMPT:], k_ext[PROMPT:]) + mask_ref[PROMPT:, PROMPT:]
            max_p = jnp.max(scores_p, axis=1, keepdims=True)
            exp_p = jnp.exp(scores_p - max_p)
            sum_p = jnp.sum(exp_p, axis=1, keepdims=True)
            out_p = dot_nn(exp_p.astype(BF), v_pair[:PROMPT]) * (1.0 / sum_p)
            max_c = jnp.maximum(
                jnp.max(scores_a, axis=1, keepdims=True), jnp.max(scores_b, axis=1, keepdims=True)
            )
            exp_a = jnp.exp(scores_a - max_c)
            exp_b = jnp.exp(scores_b - max_c)
            sum_c = jnp.sum(exp_a, axis=1, keepdims=True) + jnp.sum(exp_b, axis=1, keepdims=True)
            out_c = dot_nn(exp_a.astype(BF), v_pair[:PROMPT]) + dot_nn(
                exp_b.astype(BF), v_pair[PROMPT:]
            )
            out_c = out_c * (1.0 / sum_c)
            outs.append(jnp.concatenate([out_p, out_c], axis=0))
            lse = jnp.concatenate([max_p + jnp.log(sum_p), max_c + jnp.log(sum_c)], axis=0)
            lse_ref[...] = jnp.where(lanes == head, lse, lse_ref[...])
        attended_pairs.append(jnp.where(lanes < HEAD, outs[0], outs[1]))
    attended = jnp.concatenate(attended_pairs, axis=1)
    att_ref[...] = attended
    gated = (attended * gate).astype(BF)
    gated_ref[...] = gated
    acc_ref[...] += dot_nn(gated, wo_ref[...])

    @pl.when(step == pl.num_programs(0) - 1)
    def _():
        part_ref[...] = acc_ref[...].astype(BF)


def mlp_kernel(
    x_ref,
    own_ref,
    other_ref,
    d_ref,
    gain_ref,
    wg_ref,
    wu_ref,
    wd_ref,
    hidden_ref,
    act_ref,
    inner_ref,
    dgate_ref,
    dup_ref,
    mlp_ref,
    dact_ref,
    acc_mlp_ref,
    acc_dact_ref,
):
    step = pl.program_id(0)

    @pl.when(step == 0)
    def _():
        hidden = x_ref[...].astype(F32) + (own_ref[...].astype(F32) + other_ref[...].astype(F32))
        hidden_ref[...] = hidden
        scale = lax.rsqrt(jnp.mean(hidden * hidden, axis=1, keepdims=True) + EPS)
        act_ref[...] = (hidden * scale * gain_ref[...]).astype(BF)
        acc_mlp_ref[...] = jnp.zeros_like(acc_mlp_ref)
        acc_dact_ref[...] = jnp.zeros_like(acc_dact_ref)

    act = act_ref[...]
    gate = dot_nn(act, wg_ref[...])
    up = dot_nn(act, wu_ref[...])
    d_inner = dot_nt(d_ref[...], wd_ref[...])
    gate_sigmoid = sigmoid(gate)
    silu_value = gate * gate_sigmoid
    inner = (silu_value * up).astype(BF)
    d_gate = (d_inner * up * gate_sigmoid * (1.0 + gate * (1.0 - gate_sigmoid))).astype(BF)
    d_up = (d_inner * silu_value).astype(BF)
    inner_ref[...] = inner
    dgate_ref[...] = d_gate
    dup_ref[...] = d_up
    acc_dact_ref[...] += dot_nt(d_gate, wg_ref[...]) + dot_nt(d_up, wu_ref[...])
    acc_mlp_ref[...] += dot_nn(inner, wd_ref[...])

    @pl.when(step == pl.num_programs(0) - 1)
    def _():
        dact_ref[...] = acc_dact_ref[...].astype(BF)
        mlp_ref[...] = acc_mlp_ref[...].astype(BF)


def attn_bwd_kernel(
    x_ref,
    d_ref,
    hidden_ref,
    own_ref,
    other_ref,
    gain_ref,
    ident_row_ref,
    ident_col_ref,
    q_ref,
    k_ref,
    v_ref,
    sig_ref,
    att_ref,
    lse_ref,
    decay_ref,
    forget_ref,
    wo_ref,
    wq_ref,
    wk_ref,
    wv_ref,
    wg_ref,
    wf_ref,
    dhidden_ref,
    dattn_ref,
    gains_ref,
    dq_ref,
    dk_ref,
    dv_ref,
    dgp_ref,
    dfp_ref,
    gbias_ref,
    dact_ref,
    acc_ref,
    mask_ref,
    ddecay_ref,
):
    step = pl.program_id(0)
    lanes = lane_ids()

    @pl.when(step == 0)
    def _():
        hidden = hidden_ref[...]
        d_act = own_ref[...].astype(F32) + other_ref[...].astype(F32)
        scale = lax.rsqrt(jnp.mean(hidden * hidden, axis=1, keepdims=True) + EPS)
        weighted = d_act * gain_ref[...]
        inner_mean = jnp.mean(weighted * hidden, axis=1, keepdims=True)
        d_hidden = d_ref[...].astype(F32) + (
            scale * weighted - hidden * (scale * scale * scale) * inner_mean
        )
        dhidden_ref[...] = d_hidden
        dattn_ref[...] = d_hidden.astype(BF)
        gains_ref[0:1, :] = jnp.sum(d_act * hidden * scale, axis=0, keepdims=True)
        allowed = visible_pairs(ident_row_ref, ident_col_ref)
        mask_ref[...] = jnp.where(allowed, 0.0, NEG)
        acc_ref[...] = jnp.zeros_like(acc_ref)
        ddecay_ref[...] = jnp.zeros_like(ddecay_ref)

    d_gated = dot_nt(dattn_ref[...], wo_ref[...])
    gate = sig_ref[...]
    attended = att_ref[...]
    d_gate_pre = (d_gated * attended * gate * (1.0 - gate)).astype(BF)
    dgp_ref[...] = d_gate_pre
    d_attended = (d_gated * gate).astype(BF)
    grads_q, grads_k, grads_v = [], [], []
    for pair in range(BLOCK_HEADS // 2):
        cols = slice(pair * LANES, (pair + 1) * LANES)
        q_low = q_ref[:, cols]
        k_low = k_ref[:, cols]
        v_low = v_ref[:, cols]
        q_pair = q_low.astype(F32)
        k_pair = k_low.astype(F32)
        v_pair = v_low.astype(F32)
        do_low = d_attended[:, cols]
        do_pair = do_low.astype(F32)
        row_products = do_pair * attended[:, cols]
        dqs, dks, dvs = [], [], []
        for half in range(2):
            own = (lanes < HEAD) if half == 0 else (lanes >= HEAD)
            base = HEAD if half == 0 else 0
            head = step * BLOCK_HEADS + pair * 2 + half
            decay = column_of(lanes, decay_ref[...], head)
            lse = column_of(lanes, lse_ref[...], head)
            row_inner = jnp.sum(jnp.where(own, row_products, 0.0), axis=1, keepdims=True)
            q_ext = place_extras(
                lanes, own, q_pair * (HEAD**-0.5), base, split_three(decay - lse), 3
            )
            k_ext = place_extras(
                lanes, own, k_pair, base, [-value for value in split_three(decay)], 0
            )
            do_ext = place_extras(lanes, own, do_pair, base, split_three(-row_inner), 3)
            v_ext = place_extras(lanes, own, v_pair, base, [], 0)
            k_one = jnp.where(own, k_pair, 1.0).astype(BF)
            q_one = jnp.where(own, q_pair, 1.0).astype(BF)
            probs_p = jnp.exp(
                dot_nt(q_ext[:PROMPT], k_ext[:PROMPT]) + mask_ref[:PROMPT, :PROMPT]
            )
            probs_a = jnp.exp(dot_nt(q_ext[PROMPT:], k_ext[:PROMPT]))
            probs_b = jnp.exp(
                dot_nt(q_ext[PROMPT:], k_ext[PROMPT:]) + mask_ref[PROMPT:, PROMPT:]
            )
            ds_p = (probs_p * dot_nt(do_ext[:PROMPT], v_ext[:PROMPT])).astype(BF)
            ds_a = (probs_a * dot_nt(do_ext[PROMPT:], v_ext[:PROMPT])).astype(BF)
            ds_b = (probs_b * dot_nt(do_ext[PROMPT:], v_ext[PROMPT:])).astype(BF)
            dv_top = dot_tn(probs_p.astype(BF), do_low[:PROMPT]) + dot_tn(
                probs_a.astype(BF), do_low[PROMPT:]
            )
            dv_low = dot_tn(probs_b.astype(BF), do_low[PROMPT:])
            dk_top = dot_tn(ds_p, q_one[:PROMPT]) + dot_tn(ds_a, q_one[PROMPT:])
            dk_low = dot_tn(ds_b, q_one[PROMPT:])
            dq_top = dot_nn(ds_p, k_one[:PROMPT])
            dq_low = dot_nn(ds_a, k_one[:PROMPT]) + dot_nn(ds_b, k_one[PROMPT:])
            dvs.append(jnp.concatenate([dv_top, dv_low], axis=0))
            dks.append(jnp.concatenate([dk_top, dk_low], axis=0))
            dqs.append(jnp.concatenate([dq_top, dq_low], axis=0))
            sums = (dqs[-1] - dks[-1])[:, base : base + 1]
            ddecay_ref[...] = jnp.where(lanes == head, sums, ddecay_ref[...])
        grads_q.append(jnp.where(lanes < HEAD, dqs[0], dqs[1]) * (HEAD**-0.5))
        grads_k.append(jnp.where(lanes < HEAD, dks[0], dks[1]) * (HEAD**-0.5))
        grads_v.append(jnp.where(lanes < HEAD, dvs[0], dvs[1]))
    d_queries = jnp.concatenate(grads_q, axis=1).astype(BF)
    d_keys = jnp.concatenate(grads_k, axis=1).astype(BF)
    d_values = jnp.concatenate(grads_v, axis=1).astype(BF)
    dq_ref[...] = d_queries
    dk_ref[...] = d_keys
    dv_ref[...] = d_values
    acc_ref[...] += (
        dot_nt(d_queries, wq_ref[...])
        + dot_nt(d_keys, wk_ref[...])
        + dot_nt(d_values, wv_ref[...])
        + dot_nt(d_gate_pre, wg_ref[...])
    )

    @pl.when(step == pl.num_programs(0) - 1)
    def _():
        ancestry = jnp.where(visible_pairs(ident_row_ref, ident_col_ref), 1.0, 0.0).astype(BF)
        high, middle, low = split_three(ddecay_ref[...])
        d_log_forget = (
            dot_tn(ancestry, high.astype(BF))
            + dot_tn(ancestry, middle.astype(BF))
            + dot_tn(ancestry, low.astype(BF))
        )
        d_forget = (d_log_forget * sigmoid(-forget_ref[...])).astype(BF)
        dfp_ref[...] = d_forget
        gbias_ref[0:1, :] = jnp.sum(d_forget.astype(F32), axis=0, keepdims=True)
        d_act = (acc_ref[...] + dot_nt(d_forget, wf_ref[...])).astype(BF)
        dact_ref[...] = d_act
        x = x_ref[...].astype(F32)
        scale = lax.rsqrt(jnp.mean(x * x, axis=1, keepdims=True) + EPS)
        gains_ref[1:2, :] = jnp.sum(d_act.astype(F32) * x * scale, axis=0, keepdims=True)


def whole(shape):
    return pl.BlockSpec(shape, lambda step: (0,) * len(shape))


def rows_of(group, width):
    return pl.BlockSpec((GROUP, width), lambda step: (group, 0))


def cols_block(rows, width):
    return pl.BlockSpec((rows, width), lambda step: (0, step))


def rows_block(width, cols):
    return pl.BlockSpec((width, cols), lambda step: (step, 0))


def shape_of(rows, cols, dtype):
    return jax.ShapeDtypeStruct((rows, cols), dtype)


def cost_of(length_us):
    return pl.CostEstimate(
        flops=int(length_us * 500_000_000), bytes_accessed=100_000, transcendentals=0
    )


def params_for():
    return pltpu.CompilerParams(
        vmem_limit_bytes=60 * 1024 * 1024, dimension_semantics=("arbitrary",)
    )


def attn_forward(group, tokens, ident, gain, weights, forget_weight, forget_bias, w_out):
    width = tokens.shape[1]
    head_cols = w_out.shape[0]
    return pl.pallas_call(
        attn_fwd_kernel,
        grid=(head_cols // BLOCK_COLS,),
        in_specs=[
            rows_of(group, width),
            whole((1, GROUP)),
            whole((GROUP, 1)),
            whole((1, width)),
            cols_block(width, BLOCK_COLS),
            cols_block(width, BLOCK_COLS),
            cols_block(width, BLOCK_COLS),
            cols_block(width, BLOCK_COLS),
            whole((width, LANES)),
            whole((1, LANES)),
            rows_block(BLOCK_COLS, width),
        ],
        out_specs=[
            whole((GROUP, width)),
            whole((GROUP, width)),
            cols_block(GROUP, BLOCK_COLS),
            cols_block(GROUP, BLOCK_COLS),
            cols_block(GROUP, BLOCK_COLS),
            cols_block(GROUP, BLOCK_COLS),
            cols_block(GROUP, BLOCK_COLS),
            cols_block(GROUP, BLOCK_COLS),
            whole((GROUP, LANES)),
            whole((GROUP, LANES)),
            whole((GROUP, LANES)),
        ],
        out_shape=[
            shape_of(GROUP, width, BF),
            shape_of(GROUP, width, BF),
            shape_of(GROUP, head_cols, BF),
            shape_of(GROUP, head_cols, BF),
            shape_of(GROUP, head_cols, BF),
            shape_of(GROUP, head_cols, F32),
            shape_of(GROUP, head_cols, F32),
            shape_of(GROUP, head_cols, BF),
            shape_of(GROUP, LANES, F32),
            shape_of(GROUP, LANES, F32),
            shape_of(GROUP, LANES, F32),
        ],
        scratch_shapes=[pltpu.VMEM((GROUP, width), F32), pltpu.VMEM((GROUP, GROUP), F32)],
        compiler_params=params_for(),
        cost_estimate=cost_of(21),
        name="attn_fwd",
    )(tokens, ident[0], ident[1], gain, *weights, forget_weight, forget_bias, w_out)


def mlp_both(group, tokens, own, other, cotangent, gain, w_gate, w_up, w_down):
    width = tokens.shape[1]
    hidden_units = w_down.shape[0]
    block = 512
    return pl.pallas_call(
        mlp_kernel,
        grid=(hidden_units // block,),
        in_specs=[
            rows_of(group, width),
            whole((GROUP, width)),
            whole((GROUP, width)),
            rows_of(group, width),
            whole((1, width)),
            cols_block(width, block),
            cols_block(width, block),
            rows_block(block, width),
        ],
        out_specs=[
            whole((GROUP, width)),
            whole((GROUP, width)),
            cols_block(GROUP, block),
            cols_block(GROUP, block),
            cols_block(GROUP, block),
            whole((GROUP, width)),
            whole((GROUP, width)),
        ],
        out_shape=[
            shape_of(GROUP, width, F32),
            shape_of(GROUP, width, BF),
            shape_of(GROUP, hidden_units, BF),
            shape_of(GROUP, hidden_units, BF),
            shape_of(GROUP, hidden_units, BF),
            shape_of(GROUP, width, BF),
            shape_of(GROUP, width, BF),
        ],
        scratch_shapes=[pltpu.VMEM((GROUP, width), F32), pltpu.VMEM((GROUP, width), F32)],
        compiler_params=params_for(),
        cost_estimate=cost_of(32),
        name="mlp_both",
    )(tokens, own, other, cotangent, gain, w_gate, w_up, w_down)


def attn_backward(
    group, tokens, cotangent, hidden, own, other, gain, ident, saved, w_out, weights, forget_weight
):
    width = tokens.shape[1]
    head_cols = w_out.shape[0]
    queries, keys_low, values_low, gate, attended, lse, decay, forget_pre = saved
    return pl.pallas_call(
        attn_bwd_kernel,
        grid=(head_cols // BLOCK_COLS,),
        in_specs=[
            rows_of(group, width),
            rows_of(group, width),
            whole((GROUP, width)),
            whole((GROUP, width)),
            whole((GROUP, width)),
            whole((1, width)),
            whole((1, GROUP)),
            whole((GROUP, 1)),
            cols_block(GROUP, BLOCK_COLS),
            cols_block(GROUP, BLOCK_COLS),
            cols_block(GROUP, BLOCK_COLS),
            cols_block(GROUP, BLOCK_COLS),
            cols_block(GROUP, BLOCK_COLS),
            whole((GROUP, LANES)),
            whole((GROUP, LANES)),
            whole((GROUP, LANES)),
            rows_block(BLOCK_COLS, width),
            cols_block(width, BLOCK_COLS),
            cols_block(width, BLOCK_COLS),
            cols_block(width, BLOCK_COLS),
            cols_block(width, BLOCK_COLS),
            whole((width, LANES)),
        ],
        out_specs=[
            whole((GROUP, width)),
            whole((GROUP, width)),
            whole((8, width)),
            cols_block(GROUP, BLOCK_COLS),
            cols_block(GROUP, BLOCK_COLS),
            cols_block(GROUP, BLOCK_COLS),
            cols_block(GROUP, BLOCK_COLS),
            whole((GROUP, LANES)),
            whole((8, LANES)),
            whole((GROUP, width)),
        ],
        out_shape=[
            shape_of(GROUP, width, F32),
            shape_of(GROUP, width, BF),
            shape_of(8, width, F32),
            shape_of(GROUP, head_cols, BF),
            shape_of(GROUP, head_cols, BF),
            shape_of(GROUP, head_cols, BF),
            shape_of(GROUP, head_cols, BF),
            shape_of(GROUP, LANES, BF),
            shape_of(8, LANES, F32),
            shape_of(GROUP, width, BF),
        ],
        scratch_shapes=[
            pltpu.VMEM((GROUP, width), F32),
            pltpu.VMEM((GROUP, GROUP), F32),
            pltpu.VMEM((GROUP, LANES), F32),
        ],
        compiler_params=params_for(),
        cost_estimate=cost_of(32),
        name="attn_bwd",
    )(
        tokens,
        cotangent,
        hidden,
        own,
        other,
        gain,
        ident[0],
        ident[1],
        queries,
        keys_low,
        values_low,
        gate,
        attended,
        lse,
        decay,
        forget_pre,
        w_out,
        *weights,
        forget_weight,
    )


def grad_kernel(place_ref, extra_ref, *refs, groups, plan, order, flip):
    inputs = refs[:-3]
    keep_ref, send_ref, total_ref = refs[-3:]
    step = pl.program_id(0)
    blocks, block_rows = total_ref.shape[0], total_ref.shape[1]
    place = place_ref[0]

    def emit(left_refs, right_refs, with_extra):
        total = dot_tn(left_refs[0][...], right_refs[0][...])
        for left_ref, right_ref in zip(left_refs[1:], right_refs[1:]):
            total = total + dot_tn(left_ref[...], right_ref[...])
        if with_extra:
            total = total + extra_ref[...]
        block = total.shape[1]
        for index in range(blocks):
            total_ref[index, :, :block] = total[index * block_rows : (index + 1) * block_rows]
        for index, slot in enumerate(order):
            kept = total_ref[jnp.bitwise_xor(place, slot), :, :block]
            sent = total_ref[jnp.bitwise_xor(place, slot ^ flip), :, :block]
            keep_ref[index, :, :block] = kept.astype(BF)
            send_ref[index, :, :block] = sent.astype(BF)

    for left_at, right_at, first, count, with_extra in plan:
        pl.when(jnp.logical_and(step >= first, step < first + count))(
            functools.partial(
                emit,
                inputs[left_at : left_at + groups],
                inputs[right_at : right_at + groups],
                with_extra,
            )
        )


def half_order(bits):
    slots = [0]
    for bit in reversed(bits[1:]):
        slots = slots + [slot ^ bit for slot in slots]
    return slots


def weight_grad(products, place, devices, bits, block, extra=None):
    width = products[0][0][0].shape[1]
    groups = len(products[0][0])
    rows = width // devices
    half = devices // 2
    arrays, specs, plan, seen = [], [], [], {}
    first = 0

    def add(items, make_spec):
        at = len(arrays)
        arrays.extend(items)
        specs.extend([make_spec()] * groups)
        return at

    for index, (lefts, rights) in enumerate(products):
        if id(lefts[0]) not in seen:
            seen[id(lefts[0])] = add(lefts, lambda: rows_of(0, width))
        narrow = extra is not None and index == len(products) - 1
        cols = rights[0].shape[1]
        count = 1 if narrow else cols // block
        at = add(
            rights,
            lambda: pl.BlockSpec(
                (GROUP, cols if narrow else block),
                lambda step, first=first, count=count: (
                    0,
                    jnp.minimum(jnp.maximum(step - first, 0), count - 1),
                ),
            ),
        )
        plan.append((seen[id(lefts[0])], at, first, count, narrow))
        first += count
    if extra is None:
        extra = jnp.zeros((8, LANES), F32)
    return pl.pallas_call(
        functools.partial(
            grad_kernel, groups=groups, plan=plan, order=half_order(bits), flip=bits[0]
        ),
        grid=(first,),
        in_specs=[pl.BlockSpec(memory_space=pltpu.SMEM), whole(extra.shape)] + specs,
        out_specs=[pl.BlockSpec((half, rows, block), lambda step: (0, 0, step))] * 2,
        out_shape=[jax.ShapeDtypeStruct((half, rows, first * block), BF)] * 2,
        scratch_shapes=[pltpu.VMEM((devices, rows, block), F32)],
        compiler_params=params_for(),
        cost_estimate=cost_of(5.7 * first * block / 1024),
        name="weight_grad",
    )(place, extra, *arrays)


class SharedSum:
    def __init__(self, keep, send, bits, devices):
        self.parts, self.send, self.bits, self.devices = [keep], send, bits, devices
        self.stage = 0

    def exchange(self):
        bit = self.bits[self.stage]
        got = lax.ppermute(
            self.send, "dp", [(index, index ^ bit) for index in range(self.devices)]
        )
        self.parts.append(got)
        self.stage += 1
        remaining = got.shape[0]
        half = remaining // 2
        if self.stage < len(self.bits):
            pieces = [part[half:remaining].astype(F32) for part in self.parts]
            self.send = functools.reduce(jnp.add, pieces).astype(BF)
            self.parts = [part[:half] for part in self.parts]
        return self

    def keep(self):
        return self.parts[0]

    def result(self):
        while self.stage < len(self.bits):
            self.exchange()
        return functools.reduce(jnp.add, [part[0].astype(F32) for part in self.parts])


def after(values, *earlier):
    return lax.optimization_barrier((values, earlier))[0]


def local(
    tokens,
    cotangent,
    segments,
    gain_attn,
    w_query,
    w_key,
    w_value,
    w_outgate,
    w_forget,
    b_forget,
    w_out,
    gain_mlp,
    w_gate,
    w_up,
    w_down,
):
    devices = lax.axis_size("dp")
    place_index = lax.axis_index("dp")
    width = tokens.shape[1]
    groups = tokens.shape[0] // GROUP
    heads = w_forget.shape[1]
    rows = width // devices
    butterfly = devices & (devices - 1) == 0 and rows % 16 == 0
    place = jnp.reshape(place_index, (1,)).astype(jnp.int32)
    bits = [1 << level for level in range(devices.bit_length() - 1)]

    def swap(values):
        return lax.ppermute(values, "tensor", [(0, 1), (1, 0)])

    gain_attn_row = gain_attn[None, :]
    gain_mlp_row = gain_mlp[None, :]
    forget_weight = jnp.pad(w_forget, ((0, 0), (0, LANES - heads)))
    forget_bias = jnp.pad(b_forget, (0, LANES - heads))[None, :]
    weights = (w_query, w_key, w_value, w_outgate)
    idents = []
    for group in range(groups):
        row = jnp.concatenate([jnp.full((PROMPT,), -1, jnp.int32), segments[group]])
        idents.append((row[None, :], row[:, None]))

    def pick(source, index):
        return [source[group][index] for group in range(groups)]

    def sharing(products, block, extra=None):
        return SharedSum(
            *weight_grad(products, place, devices, bits, block, extra), bits, devices
        )

    def scattered(lefts, rights):
        total = functools.reduce(
            jnp.add, [dot_tn(left, right) for left, right in zip(lefts, rights)]
        )
        return lax.psum_scatter(total, "dp", scatter_dimension=0, tiled=True)

    def forward_of(group, rows_in):
        return attn_forward(
            group,
            rows_in,
            idents[group],
            gain_attn_row,
            weights,
            forget_weight,
            forget_bias,
            w_out,
        )

    def middle_of(group, own):
        return mlp_both(
            group,
            tokens,
            own,
            attn_other[group],
            cotangent,
            gain_mlp_row,
            w_gate,
            w_up,
            w_down,
        )

    def backward_of(group, own):
        (_, _, queries, keys_low, values_low, gate, attended, _, lse, decay, forget_pre) = forward[
            group
        ]
        return attn_backward(
            group,
            tokens,
            cotangent,
            middle[group][0],
            own,
            dact_other[group],
            gain_mlp_row,
            idents[group],
            (queries, keys_low, values_low, gate, attended, lse, decay, forget_pre),
            w_out,
            weights,
            forget_weight,
        )

    forward = []
    for group in range(groups):
        earlier = () if group == 0 else (forward[-1][0],)
        forward.append(forward_of(group, after(tokens, *earlier)))
    attn_other = [swap(forward[group][0]) for group in range(groups)]
    middle = []
    for group in range(groups):
        earlier = () if group == 0 else (middle[-1][6],)
        middle.append(middle_of(group, after(forward[group][0], *earlier)))
    dact_other = []
    for group in range(groups):
        earlier = () if group == 0 else (dact_other[-1],)
        dact_other.append(swap(after(middle[group][6], *earlier)))
    mlp_other = []
    for group in range(groups):
        earlier = (dact_other[-1],) if group == 0 else (mlp_other[-1],)
        mlp_other.append(swap(after(middle[group][5], *earlier)))
    results = [
        (
            middle[group][0] + (middle[group][5].astype(F32) + mlp_other[group].astype(F32))
        ).astype(BF)
        for group in range(groups)
    ]
    d_rows = [cotangent[group * GROUP : (group + 1) * GROUP] for group in range(groups)]
    acts_mlp = pick(middle, 1)
    acts_attn = pick(forward, 1)
    sums = {}
    before = {group: () for group in range(groups)}
    if butterfly:
        sum_gate = sharing([(acts_mlp, pick(middle, 3))], 512)
        sum_gate.send = after(sum_gate.send, dact_other[0])
        sum_up = sharing([(acts_mlp, after(pick(middle, 4), sum_gate.keep()))], 512)
        sum_gate.exchange()
        before[0] = (sum_up.send, sum_gate.send)
    else:
        sums["gate"] = scattered(acts_mlp, pick(middle, 3))
        sums["up"] = scattered(acts_mlp, pick(middle, 4))
        sums["down"] = scattered(d_rows, pick(middle, 2))
    backward = []
    for group in range(groups):
        backward.append(backward_of(group, after(middle[group][6], *before[group])))
        if butterfly and group == 0:
            inners = after(pick(middle, 2), backward[0][9])
            sum_down = sharing([(d_rows, inners)], 512)
            sum_gate.exchange()
            sum_up.exchange()
            before[1] = (sum_gate.send, sum_up.send, sum_down.send)
    dtok_other = [swap(backward[group][9]) for group in range(groups)]
    d_tokens = []
    for group in range(groups):
        x = tokens[group * GROUP : (group + 1) * GROUP].astype(F32)
        scale = lax.rsqrt(jnp.mean(x * x, axis=1, keepdims=True) + EPS)
        d_act = backward[group][9].astype(F32) + dtok_other[group].astype(F32)
        weighted = d_act * gain_attn_row
        inner_mean = jnp.mean(weighted * x, axis=1, keepdims=True)
        d_tokens.append(
            (
                backward[group][0] + (scale * weighted - x * (scale * scale * scale) * inner_mean)
            ).astype(BF)
        )

    gains = functools.reduce(jnp.add, pick(backward, 2))
    g_bias = functools.reduce(jnp.add, pick(backward, 8))[0, :heads]
    gain_attn_sum = gains[1] + swap(gains[1])
    extra = jnp.concatenate(
        [
            jnp.zeros((width, heads), F32),
            gains[0][:, None],
            gain_attn_sum[:, None],
            jnp.broadcast_to(g_bias[None, :], (width, heads)),
            jnp.zeros((width, LANES - 2 - 2 * heads), F32),
        ],
        axis=1,
    )
    dattns = pick(backward, 1)
    gateds = pick(forward, 7)
    forget_grads = pick(backward, 7)
    if butterfly:
        head_cols = w_out.shape[0]
        block = 384
        sum_down.exchange()
        sum_up.exchange()
        sum_gate.exchange()
        first_acts, first_dattns = after(
            (acts_attn, dattns), sum_up.send, sum_gate.send, sum_down.send, results[0]
        )
        first = sharing(
            [
                (first_dattns, gateds),
                (first_acts, pick(backward, 3)),
                (first_acts, pick(backward, 4)),
            ],
            block,
        )
        sum_down.exchange()
        second = sharing(
            [
                (acts_attn, pick(backward, 5)),
                (acts_attn, pick(backward, 6)),
                (acts_attn, after(forget_grads, sum_down.send, first.send, dtok_other[0])),
            ],
            block,
            extra,
        )
        first.exchange()
        first.send = after(first.send, second.send)
        sums["gate"], sums["up"], sums["down"] = [
            one.result() for one in (sum_gate, sum_up, sum_down)
        ]
        total = first.result()
        sums["out"], sums["query"], sums["key"] = [
            total[:, index * head_cols : (index + 1) * head_cols] for index in range(3)
        ]
        total = second.result()
        sums["value"], sums["outgate"] = [
            total[:, index * head_cols : (index + 1) * head_cols] for index in range(2)
        ]
        small_sum = total[:, 2 * head_cols : 2 * head_cols + LANES]
    else:
        sums["out"] = scattered(dattns, gateds)
        for index, name in enumerate(("query", "key", "value", "outgate")):
            sums[name] = scattered(acts_attn, pick(backward, 3 + index))
        g_forget = functools.reduce(
            jnp.add, [dot_tn(left, right) for left, right in zip(acts_attn, forget_grads)]
        )
        small_sum = lax.psum_scatter(g_forget + extra, "dp", scatter_dimension=0, tiled=True)
    return (
        jnp.concatenate(results, axis=0),
        jnp.concatenate(d_tokens, axis=0),
        small_sum[:, heads + 1],
        sums["query"],
        sums["key"],
        sums["value"],
        sums["outgate"],
        small_sum[:, :heads],
        small_sum[0, heads + 2 : 2 * heads + 2],
        sums["out"].T,
        small_sum[:, heads],
        sums["gate"],
        sums["up"],
        sums["down"].T,
    )


def solution(mesh):
    in_specs = (
        P("dp", None),
        P("dp", None),
        P("dp", None),
        P(),
        P(None, "tensor"),
        P(None, "tensor"),
        P(None, "tensor"),
        P(None, "tensor"),
        P(None, "tensor"),
        P("tensor"),
        P("tensor", None),
        P(),
        P(None, "tensor"),
        P(None, "tensor"),
        P("tensor", None),
    )
    out_specs = (
        P("dp", None),
        P("dp", None),
        P("dp"),
        P("dp", "tensor"),
        P("dp", "tensor"),
        P("dp", "tensor"),
        P("dp", "tensor"),
        P("dp", "tensor"),
        P("tensor"),
        P("tensor", "dp"),
        P("dp"),
        P("dp", "tensor"),
        P("dp", "tensor"),
        P("tensor", "dp"),
    )
    return jax.shard_map(local, mesh=mesh, in_specs=in_specs, out_specs=out_specs, check_vma=False)
```

time: 1630 us -> 527 us (0.32)
  waiting for transfers between devices: 1080 us -> 162 us
  matrix products: 317 us -> 0 us
  Pallas kernels: 0 us -> 249 us
  blocking collectives: 70.8 us -> 0 us
  local copies, waits for them, and re-layouts: 75.3 us -> 25.5 us
  starting transfers between devices: 1.51 us -> 28.9 us
    reduce_scatter x16 -> x0, waiting for transfers between devices: 915 us -> none  [the longest x1 138 us: local(): lax.psum_scatter(t_up, 'dp', scatter_dimension=0, tiled=True)]
    dot_general x70 -> x0, matrix products: 317 us -> none  [the longest x18 107 us: contract_rows(): lax.dot_general(first_arg, second_arg, (((0,), (0,)), ((), ())), preferre...]
    pallas_call x0 -> x11, Pallas kernels: none -> 249 us  [the longest x5 77.8 us: weight_grad(): pl.pallas_call(functools.partial(grad_kernel, groups=groups, plan=plan, o...]
    ppermute x0 -> x29, waiting for transfers between devices: none -> 162 us  [the longest x20 124 us: exchange(): lax.ppermute(self.send, 'dp', [(index, index ^ bit) for index in range(se...]
    all_gather x8 -> x0, waiting for transfers between devices: 160 us -> none  [the longest x2 54.6 us: micro_step(): act_mlp = lax.all_gather(act_share, 'tensor', axis=0, tiled=True)]
    psum x2 -> x0, blocking collectives: 70.8 us -> none  [the longest x1 37 us: local(): lax.psum((gain_local[0], gain_local[1]), ('dp', 'tensor'))]
    while x198 -> x0, local copies, waits for them, and re-layouts: 31.4 us -> none  [the longest x2 18.9 us: local(): lax.fori_loop(0, MICRO, step_end, (empty_outputs, zero_grads))]
    ppermute x0 -> x29, starting transfers between devices: none -> 28.9 us  [the longest x20 19.1 us: exchange(): lax.ppermute(self.send, 'dp', [(index, index ^ bit) for index in range(se...]
  transfers between devices with their start and end apart: 25 -> 29, of which waited for: 21 -> 13; matrix products, arithmetic and copies ran while one was open for 10% -> 13% of each run, Pallas kernels for 0% -> 43%
where the time goes in v1:
time: 527 us; the launch traced here: 523 us
  Pallas kernels  249 us (47%)
  waiting for transfers between devices  162 us (31%)
  other arithmetic  56.5 us (11%)
  starting transfers between devices  28.9 us (5%)
  local copies, waits for them, and re-layouts  25.5 us (5%)
    ppermute x20, waiting for transfers between devices, exchange(): lax.ppermute(self.send, 'dp', [(index, index ^ bit) for index in range(se...  124 us
    pallas_call x5, Pallas kernels, weight_grad(): pl.pallas_call(functools.partial(grad_kernel, groups=groups, plan=plan, o...  77.8 us
    pallas_call x2, Pallas kernels, mlp_both(): pl.pallas_call(mlp_kernel, grid=(hidden_units // block,), in_specs=[rows_...  64.1 us
    pallas_call x2, Pallas kernels, attn_backward(): pl.pallas_call(attn_bwd_kernel, grid=(head_cols // BLOCK_COLS,), in_specs...  64.1 us
    pallas_call x2, Pallas kernels, attn_forward(): pl.pallas_call(attn_fwd_kernel, grid=(head_cols // BLOCK_COLS,), in_specs...  42.5 us
    ppermute x9, waiting for transfers between devices, swap(): return lax.ppermute(values, 'tensor', [(0, 1), (1, 0)])  38.1 us
    convert_element_type x15, other arithmetic, exchange(): self.send = functools.reduce(jnp.add, pieces).astype(BF)  27.2 us
    ppermute x20, starting transfers between devices, exchange(): lax.ppermute(self.send, 'dp', [(index, index ^ bit) for index in range(se...  19.1 us
  transfers between devices with their start and end apart: 29, of which 13 were waited for; matrix products, arithmetic and copies ran while one was open for 13% of the time, Pallas kernels for 43%

profile of v1, /device:TPU:0, one launch (start us, length us, event | category | flops | bytes accessed | tf_op | source)
XLA Modules:
  0.0 522.9 jit_solution(4324359056068830861)
XLA Ops:
  3.3 1.3 broadcast_in_dim.43.gain_ref
  4.6 1.2 pad_bitcast_fusion.bias_ref
  6.7 21.2 %attn_fwd.2 = (bf16[512,1536]{1,0:T(8,128)(2,1)}, bf16[512,1536]{1,0:T(8,128)(2,1)}, bf16[512,768]{1,0:T(8,128)(2,1)}, bf16[512,768]{1,0:T(8,128)(2,1)}, bf16[51...) custom-call(bf16[1024,1536]{1,0:T(8,128)(2,1)} %x_ref.9, ...), custom_call_target="tpu_custom_call" | custom-call | flops 10499999744 | bytes 100000 | tf_op jit(solution)/shard_map/attn_fwd/pallas_call | solution.py:425
  27.9 3.0 collective-permute-start
  31.8 21.2 %attn_fwd.3 = (bf16[512,1536]{1,0:T(8,128)(2,1)}, bf16[512,1536]{1,0:T(8,128)(2,1)}, bf16[512,768]{1,0:T(8,128)(2,1)}, bf16[512,768]{1,0:T(8,128)(2,1)}, bf16[51...) custom-call(bf16[1024,1536]{1,0:T(8,128)(2,1)} %x_ref.9, ...), custom_call_target="tpu_custom_call" | custom-call | flops 10499999744 | bytes 100000 | tf_op jit(solution)/shard_map/attn_fwd/pallas_call | solution.py:425
  53.7 12.6 %collective-permute-done.other_ref = bf16[512,1536]{1,0:T(8,128)(2,1)S(1)} collective-permute-done((bf16[512,1536]{1,0:T(8,128)(2,1)}, bf16[512,1536]{1,0:T(8,128)(2,1)S(1)}, u32[]{:S(2)}, u32[]{:S(2)}) %collective-permute-start) | collective-permute-done | bytes 1572896 | tf_op jit(solution)/shard_map/ppermute | solution.py:754
  66.4 1.2 copy-done.24
  67.6 32.4 %mlp_both.2 = (f32[512,1536]{1,0:T(8,128)}, bf16[512,1536]{1,0:T(8,128)(2,1)}, bf16[512,2048]{1,0:T(8,128)(2,1)}, bf16[512,2048]{1,0:T(8,128)(2,1)}, bf16[512,20...) custom-call(bf16[1024,1536]{1,0:T(8,128)(2,1)} %x_ref.9, ...), custom_call_target="tpu_custom_call" | custom-call | flops 16000000000 | bytes 100000 | tf_op jit(solution)/shard_map/mlp_both/pallas_call | solution.py:478
  100.0 2.1 collective-permute-start.2
  102.1 31.7 %mlp_both.3 = (f32[512,1536]{1,0:T(8,128)}, bf16[512,1536]{1,0:T(8,128)(2,1)}, bf16[512,2048]{1,0:T(8,128)(2,1)}, bf16[512,2048]{1,0:T(8,128)(2,1)}, bf16[512,20...) custom-call(bf16[1024,1536]{1,0:T(8,128)(2,1)} %x_ref.9, ...), custom_call_target="tpu_custom_call" | custom-call | flops 16000000000 | bytes 100000 | tf_op jit(solution)/shard_map/mlp_both/pallas_call | solution.py:478
  134.5 23.4 %weight_grad.5 = (bf16[8,96,2048]{2,1,0:T(8,128)(2,1)}, bf16[8,96,2048]{2,1,0:T(8,128)(2,1)}) custom-call(s32[1]{0:T(128)} %bitcast.7.place_ref, f32[8,128]{1,0:T(8,128)} %broadcast_6_extra_ref.2.extra_ref, bf16[512,1536]{1,0:T(8,128)(2,1)} %get-tuple-element.112.refs_0_, bf16[512,1536]{1,0:T(8,128)(2,1)} %get-tuple-element.113.refs_1_, ...), custom_call_target="tpu_custom_call" | custom-call | flops 5699999744 | bytes 100000 | tf_op jit(solution)/shard_map/weight_grad/pallas_call | solution.py:678
  157.9 11.7 %weight_grad.6 = (bf16[8,96,2048]{2,1,0:T(8,128)(2,1)}, bf16[8,96,2048]{2,1,0:T(8,128)(2,1)}) custom-call(s32[1]{0:T(128)} %bitcast.7.place_ref, f32[8,128]{1,0:T(8,128)} %broadcast_6_extra_ref.2.extra_ref, bf16[512,1536]{1,0:T(8,128)(2,1)} %get-tuple-element.112.refs_0_, bf16[512,1536]{1,0:T(8,128)(2,1)} %get-tuple-element.113.refs_1_, ...), custom_call_target="tpu_custom_call" | custom-call | flops 5699999744 | bytes 100000 | tf_op jit(solution)/shard_map/weight_grad/pallas_call | solution.py:678
  170.1 5.3 %collective-permute-done.9 = bf16[8,96,2048]{2,1,0:T(8,128)(2,1)S(1)} collective-permute-done((bf16[8,96,2048]{2,1,0:T(8,128)(2,1)}, bf16[8,96,2048]{2,1,0:T(8,128)(2,1)S(1)}, u32[]{:S(2)}, u32[]{:S(2)}) %collective-permute-start.9) | collective-permute-done | bytes 3145760 | tf_op jit(solution)/shard_map/ppermute | solution.py:700
  175.5 3.1 add_convert_fusion.2
  178.6 1.6 collective-permute-start.14
  180.2 1.8 fusion.12
  182.0 24.5 %collective-permute-done.3.other_ref = bf16[512,1536]{1,0:T(8,128)(2,1)S(1)} collective-permute-done((bf16[512,1536]{1,0:T(8,128)(2,1)S(1)}, bf16[512,1536]{1,0:T(8,128)(2,1)S(1)}, u32[]{:S(2)}, u32[]{:S(2)}) %collective-permute-start.3) | collective-permute-done | bytes 1572896 | tf_op jit(solution)/shard_map/ppermute | solution.py:754
  206.8 2.3 add_convert_fusion.3
  209.1 1.7 collective-permute-start.8
  210.8 5.1 collective-permute-done.14
  215.9 3.0 add_convert_fusion.8
  218.9 1.6 collective-permute-start.25
  220.5 31.9 %attn_bwd.2 = (f32[512,1536]{1,0:T(8,128)}, bf16[512,1536]{1,0:T(8,128)(2,1)}, f32[8,1536]{1,0:T(8,128)}, bf16[512,768]{1,0:T(8,128)(2,1)}, bf16[512,768]{1,0:T(...) custom-call(bf16[1024,1536]{1,0:T(8,128)(2,1)} %x_ref.9, ...), custom_call_target="tpu_custom_call" | custom-call | flops 16000000000 | bytes 100000 | tf_op jit(solution)/shard_map/attn_bwd/pallas_call | solution.py:522
  253.0 11.9 %weight_grad.7 = (bf16[8,96,2048]{2,1,0:T(8,128)(2,1)}, bf16[8,96,2048]{2,1,0:T(8,128)(2,1)}) custom-call(s32[1]{0:T(128)} %bitcast.7.place_ref, f32[8,128]{1,0:T(8,128)} %broadcast_6_extra_ref.2.extra_ref, bf16[512,1536]{1,0:T(8,128)(2,1)} %get-tuple-element.221.refs_0_, bf16[512,1536]{1,0:T(8,128)(2,1)} %get-tuple-element.220.refs_1_, ...), custom_call_target="tpu_custom_call" | custom-call | flops 5699999744 | bytes 100000 | tf_op jit(solution)/shard_map/weight_grad/pallas_call | solution.py:678
  265.0 1.6 collective-permute-start.5
  266.6 1.5 add_convert_fusion.14
  268.1 2.7 collective-permute-start.26
  270.7 3.4 add_convert_fusion.5
  274.2 14.3 %collective-permute-done.26 = bf16[1,96,2048]{2,1,0:T(8,128)(2,1)S(1)} collective-permute-done((bf16[1,96,2048]{2,1,0:T(8,128)(2,1)S(1)}, bf16[1,96,2048]{2,1,0:T(8,128)(2,1)S(1)}, u32[]{:S(2)}, u32[]{:S(2)}) %collective-permute-start.26) | collective-permute-done | bytes 393248 | tf_op jit(solution)/shard_map/ppermute | solution.py:700
  288.5 2.5 add_bitcast_fusion.2
  291.0 2.9 add_convert_fusion.10
  293.9 32.2 %attn_bwd.3 = (f32[512,1536]{1,0:T(8,128)}, bf16[512,1536]{1,0:T(8,128)(2,1)}, f32[8,1536]{1,0:T(8,128)}, bf16[512,768]{1,0:T(8,128)(2,1)}, bf16[512,768]{1,0:T(...) custom-call(bf16[1024,1536]{1,0:T(8,128)(2,1)} %x_ref.9, ...), custom_call_target="tpu_custom_call" | custom-call | flops 16000000000 | bytes 100000 | tf_op jit(solution)/shard_map/attn_bwd/pallas_call | solution.py:522
  327.5 1.6 add_convert_fusion.15
  329.1 3.7 add_convert_fusion.1
  332.8 1.5 collective-permute-start.13
  334.3 17.2 %weight_grad.8 = (bf16[8,96,2304]{2,1,0:T(8,128)(2,1)}, bf16[8,96,2304]{2,1,0:T(8,128)(2,1)}) custom-call(s32[1]{0:T(128)} %bitcast.7.place_ref, f32[8,128]{1,0:T(8,128)} %broadcast_6_extra_ref.2.extra_ref, bf16[512,1536]{1,0:T(8,128)(2,1)} %get-tuple-element.167.refs_0_, bf16[512,1536]{1,0:T(8,128)(2,1)} %get-tuple-element.168.refs_1_, ...), custom_call_target="tpu_custom_call" | custom-call | flops 6412499968 | bytes 100000 | tf_op jit(solution)/shard_map/weight_grad/pallas_call | solution.py:678
  351.5 3.5 add_convert_fusion.4
  355.0 3.2 collective-permute-start.24
  358.2 1.9 pad_maximum_fusion
  360.1 1.6 collective-permute-start.10
  363.5 1.6 broadcast_in_dim.51
  366.9 3.8 concatenate.19.extra_ref
  370.7 5.8 %collective-permute-done.24 = bf16[1,96,2048]{2,1,0:T(8,128)(2,1)} collective-permute-done((bf16[1,96,2048]{2,1,0:T(8,128)(2,1)S(1)}, bf16[1,96,2048]{2,1,0:T(8,128)(2,1)}, u32[]{:S(2)}, u32[]{:S(2)}) %collective-permute-start.24) | collective-permute-done | bytes 393248 | tf_op jit(solution)/shard_map/ppermute | solution.py:700
  376.5 2.6 add_bitcast_fusion.3
  379.2 2.0 add_convert_fusion.9
  381.2 1.1 copy-done.2
  382.3 13.6 %weight_grad.9 = (bf16[8,96,1920]{2,1,0:T(8,128)(2,1)}, bf16[8,96,1920]{2,1,0:T(8,128)(2,1)}) custom-call(s32[1]{0:T(128)} %bitcast.7.place_ref, f32[1536,128]{1,0:T(8,128)} %concatenate.19.extra_ref, bf16[512,1536]{1,0:T(8,128)(2,1)} %get-tuple-element.171.refs_4_.refs_0_, bf16[512,1536]{1,0:T(8,128)(2,1)} %get-tuple-element.172.refs_5_.refs_1_, ...), custom_call_target="tpu_custom_call" | custom-call | flops 5343750144 | bytes 100000 | tf_op jit(solution)/shard_map/weight_grad/pallas_call | solution.py:678
  397.0 4.1 fusion.5
  401.2 2.1 add_convert_fusion
  403.9 4.0 fusion.4
  407.9 1.9 pad_maximum_fusion.1
  411.2 1.6 collective-permute-start.17
  412.8 14.1 %collective-permute-done.27 = bf16[2,96,2048]{2,1,0:T(8,128)(2,1)S(1)} collective-permute-done((bf16[2,96,2048]{2,1,0:T(8,128)(2,1)S(1)}, bf16[2,96,2048]{2,1,0:T(8,128)(2,1)S(1)}, u32[]{:S(2)}, u32[]{:S(2)}) %collective-permute-start.27) | collective-permute-done | bytes 786464 | tf_op jit(solution)/shard_map/ppermute | solution.py:700
  426.9 1.5 add_convert_fusion.13
  429.2 15.6 %collective-permute-done.21 = bf16[4,96,2304]{2,1,0:T(8,128)(2,1)S(1)} collective-permute-done((bf16[4,96,2304]{2,1,0:T(8,128)(2,1)S(1)}, bf16[4,96,2304]{2,1,0:T(8,128)(2,1)S(1)}, u32[]{:S(2)}, u32[]{:S(2)}) %collective-permute-start.21) | collective-permute-done | bytes 1769504 | tf_op jit(solution)/shard_map/ppermute | solution.py:700
  444.8 1.5 add_convert_fusion.7
  446.4 1.1 collective-permute-done.28
  447.5 2.4 add_bitcast_fusion.1
  449.9 25.2 %collective-permute-done.17 = bf16[4,96,1920]{2,1,0:T(8,128)(2,1)S(1)} collective-permute-done((bf16[4,96,1920]{2,1,0:T(8,128)(2,1)S(1)}, bf16[4,96,1920]{2,1,0:T(8,128)(2,1)S(1)}, u32[]{:S(2)}, u32[]{:S(2)}) %collective-permute-start.17) | collective-permute-done | bytes 1474592 | tf_op jit(solution)/shard_map/ppermute | solution.py:700
  475.5 1.2 add_convert_fusion.12
  476.8 2.5 collective-permute-start.23
  479.3 22.9 %collective-permute-done.18 = bf16[2,96,1920]{2,1,0:T(8,128)(2,1)S(1)} collective-permute-done((bf16[2,96,1920]{2,1,0:T(8,128)(2,1)S(1)}, bf16[2,96,1920]{2,1,0:T(8,128)(2,1)S(1)}, u32[]{:S(2)}, u32[]{:S(2)}) %collective-permute-start.18) | collective-permute-done | bytes 737312 | tf_op jit(solution)/shard_map/ppermute | solution.py:700
  502.9 1.3 add_bitcast_fusion
  505.1 14.6 %collective-permute-done.19 = bf16[1,96,1920]{2,1,0:T(8,128)(2,1)S(1)} collective-permute-done((bf16[1,96,1920]{2,1,0:T(8,128)(2,1)S(1)}, bf16[1,96,1920]{2,1,0:T(8,128)(2,1)S(1)}, u32[]{:S(2)}, u32[]{:S(2)}) %collective-permute-start.19) | collective-permute-done | bytes 368672 | tf_op jit(solution)/shard_map/ppermute | solution.py:700
  (112 shorter events, 21.3 us)
Async XLA Ops:
  2.5 4.2 copy-start.16
  27.9 38.5 %collective-permute-start = (bf16[512,1536]{1,0:T(8,128)(2,1)}, bf16[512,1536]{1,0:T(8,128)(2,1)S(1)}, u32[]{:S(2)}, u32[]{:S(2)}) collective-permute-start(bf16[512,1536]{1,0:T(8,128)(2,1)} %get-tuple-element.99.own_ref), channel_id=1, source_target_pairs={{0,1},{1,0},{2,3},{3,2},{4,5},{5,4},{6,7},{7,6},{8,9},{9,8},{10,11... | collective-permute-start | bytes 4718600 | tf_op jit(solution)/shard_map/ppermute | solution.py:754
  30.9 0.9 copy-start.15
  31.8 21.4 %copy-start.18 = (f32[1536]{0:T(1024)S(1)}, f32[1536]{0:T(1024)}, u32[]{:S(2)}) copy-start(f32[1536]{0:T(1024)} %param.26) | copy-start | bytes 18436
  53.0 49.1 %collective-permute-start.1 = (bf16[512,1536]{1,0:T(8,128)(2,1)}, bf16[512,1536]{1,0:T(8,128)(2,1)}, u32[]{:S(2)}, u32[]{:S(2)}) collective-permute-start(bf16[512,1536]{1,0:T(8,128)(2,1)} %get-tuple-element.105.own_ref), channel_id=1, source_target_pairs={{0,1},{1,0},{2,3},{3,2},{4,5},{5,4},{6,7},{7,6},{8,9},{9,8},{10,11... | collective-permute-start | bytes 4718600 | tf_op jit(solution)/shard_map/ppermute | solution.py:754
  66.4 1.2 copy-start.24
  100.0 69.6 %collective-permute-start.2 = (bf16[512,1536]{1,0:T(8,128)(2,1)}, bf16[512,1536]{1,0:T(8,128)(2,1)S(1)}, u32[]{:S(2)}, u32[]{:S(2)}) collective-permute-start(bf16[512,1536]{1,0:T(8,128)(2,1)} %get-tuple-element.124.own_ref), channel_id=1, source_target_pairs={{0,1},{1,0},{2,3},{3,2},{4,5},{5,4},{6,7},{7,6},{8,9},{9,8},{10,11... | collective-permute-start | bytes 4718600 | tf_op jit(solution)/shard_map/ppermute | solution.py:754
  157.9 12.2 %copy-start.21 = (bf16[512,1536]{1,0:T(8,128)(2,1)S(1)}, bf16[512,1536]{1,0:T(8,128)(2,1)}, u32[]{:S(2)}) copy-start(bf16[512,1536]{1,0:T(8,128)(2,1)} %get-tuple-element.141.own_ref) | copy-start | bytes 4718596
  169.6 10.6 %copy-start.5 = (bf16[1024,1536]{1,0:T(8,128)(2,1)S(1)}, bf16[1024,1536]{1,0:T(8,128)(2,1)}, u32[]{:S(2)}) copy-start(bf16[1024,1536]{1,0:T(8,128)(2,1)} %d_ref.7) | copy-start | bytes 9437188
  169.6 5.9 %collective-permute-start.9 = (bf16[8,96,2048]{2,1,0:T(8,128)(2,1)}, bf16[8,96,2048]{2,1,0:T(8,128)(2,1)S(1)}, u32[]{:S(2)}, u32[]{:S(2)}) collective-permute-start(bf16[8,96,2048]{2,1,0:T(8,128)(2,1)} %get-tuple-element.121), channel_id=1, source_target_pairs={{0,2},{2,0},{4,6},{6,4},{8,10},{10,8},{12,14},{14,12},{16,18},{18,... | collective-permute-start | bytes 9437192 | tf_op jit(solution)/shard_map/ppermute | solution.py:700
  169.6 5.9 %copy-start.23 = (bf16[512,1536]{1,0:T(8,128)(2,1)}, bf16[512,1536]{1,0:T(8,128)(2,1)S(1)}, u32[]{:S(2)}) copy-start(bf16[512,1536]{1,0:T(8,128)(2,1)S(1)} %collective-permute-done.2.other_ref) | copy-start | bytes 4718596
  169.6 37.2 %collective-permute-start.6 = (bf16[8,96,2048]{2,1,0:T(8,128)(2,1)}, bf16[8,96,2048]{2,1,0:T(8,128)(2,1)S(1)}, u32[]{:S(2)}, u32[]{:S(2)}) collective-permute-start(bf16[8,96,2048]{2,1,0:T(8,128)(2,1)} %get-tuple-element.123), channel_id=1, source_target_pairs={{0,2},{2,0},{4,6},{6,4},{8,10},{10,8},{12,14},{14,12},{16,18},{18,... | collective-permute-start | bytes 9437192 | tf_op jit(solution)/shard_map/ppermute | solution.py:700
  170.1 36.4 %collective-permute-start.3 = (bf16[512,1536]{1,0:T(8,128)(2,1)S(1)}, bf16[512,1536]{1,0:T(8,128)(2,1)S(1)}, u32[]{:S(2)}, u32[]{:S(2)}) collective-permute-start(bf16[512,1536]{1,0:T(8,128)(2,1)S(1)} %copy-done.21), channel_id=1, source_target_pairs={{0,1},{1,0},{2,3},{3,2},{4,5},{5,4},{6,7},{7,6},{8,9},{9,8},{10,11... | collective-permute-start | bytes 4718600 | tf_op jit(solution)/shard_map/ppermute | solution.py:754
  175.4 40.5 %copy-start.8 = (bf16[8,96,2048]{2,1,0:T(8,128)(2,1)}, bf16[8,96,2048]{2,1,0:T(8,128)(2,1)S(1)}, u32[]{:S(2)}) copy-start(bf16[8,96,2048]{2,1,0:T(8,128)(2,1)S(1)} %collective-permute-done.9) | copy-start | bytes 9437188
  178.6 28.2 %copy-start.6 = (bf16[8,96,2048]{2,1,0:T(8,128)(2,1)S(1)}, bf16[8,96,2048]{2,1,0:T(8,128)(2,1)}, u32[]{:S(2)}) copy-start(bf16[8,96,2048]{2,1,0:T(8,128)(2,1)} %get-tuple-element.118) | copy-start | bytes 9437188
  178.6 37.3 %collective-permute-start.14 = (bf16[4,96,2048]{2,1,0:T(8,128)(2,1)S(1)}, bf16[4,96,2048]{2,1,0:T(8,128)(2,1)S(1)}, u32[]{:S(2)}, u32[]{:S(2)}) collective-permute-start(bf16[4,96,2048]{2,1,0:T(8,128)(2,1)S(1)} %add_convert_fusion.2), channel_id=1, source_target_pairs={{0,4},{2,6},{4,0},{6,2},{8,12},{10,14},{12,8},{14,10},{16,20},{18,... | collective-permute-start | bytes 4718600 | tf_op jit(solution)/shard_map/ppermute | solution.py:700
  206.5 12.4 %copy-start.22 = (bf16[512,1536]{1,0:T(8,128)(2,1)}, bf16[512,1536]{1,0:T(8,128)(2,1)S(1)}, u32[]{:S(2)}) copy-start(bf16[512,1536]{1,0:T(8,128)(2,1)S(1)} %collective-permute-done.3.other_ref) | copy-start | bytes 4718596
  206.5 58.5 %collective-permute-start.4 = (bf16[512,1536]{1,0:T(8,128)(2,1)}, bf16[512,1536]{1,0:T(8,128)(2,1)}, u32[]{:S(2)}, u32[]{:S(2)}) collective-permute-start(bf16[512,1536]{1,0:T(8,128)(2,1)} %get-tuple-element.108), channel_id=1, source_target_pairs={{0,1},{1,0},{2,3},{3,2},{4,5},{5,4},{6,7},{7,6},{8,9},{9,8},{10,11... | collective-permute-start | bytes 4718600 | tf_op jit(solution)/shard_map/ppermute | solution.py:754
  206.8 12.1 %copy-start.7 = (bf16[8,96,2048]{2,1,0:T(8,128)(2,1)}, bf16[8,96,2048]{2,1,0:T(8,128)(2,1)S(1)}, u32[]{:S(2)}) copy-start(bf16[8,96,2048]{2,1,0:T(8,128)(2,1)S(1)} %collective-permute-done.6) | copy-start | bytes 9437188
  209.1 81.9 %collective-permute-start.8 = (bf16[4,96,2048]{2,1,0:T(8,128)(2,1)}, bf16[4,96,2048]{2,1,0:T(8,128)(2,1)}, u32[]{:S(2)}, u32[]{:S(2)}) collective-permute-start(bf16[4,96,2048]{2,1,0:T(8,128)(2,1)} %add_convert_fusion.3), channel_id=1, source_target_pairs={{0,4},{2,6},{4,0},{6,2},{8,12},{10,14},{12,8},{14,10},{16,20},{18,... | collective-permute-start | bytes 4718600 | tf_op jit(solution)/shard_map/ppermute | solution.py:700
  215.9 50.7 %copy-start.12 = (bf16[4,96,2048]{2,1,0:T(8,128)(2,1)}, bf16[4,96,2048]{2,1,0:T(8,128)(2,1)S(1)}, u32[]{:S(2)}) copy-start(bf16[4,96,2048]{2,1,0:T(8,128)(2,1)S(1)} %collective-permute-done.14) | copy-start | bytes 4718596
  218.9 47.7 %collective-permute-start.25 = (bf16[2,96,2048]{2,1,0:T(8,128)(2,1)}, bf16[2,96,2048]{2,1,0:T(8,128)(2,1)}, u32[]{:S(2)}, u32[]{:S(2)}) collective-permute-start(bf16[2,96,2048]{2,1,0:T(8,128)(2,1)} %add_convert_fusion.8), channel_id=1, source_target_pairs={{0,8},{2,10},{4,12},{6,14},{8,0},{10,2},{12,4},{14,6},{16,24},{18,... | collective-permute-start | bytes 2359304 | tf_op jit(solution)/shard_map/ppermute | solution.py:700
  252.4 128.7 %collective-permute-start.7 = (bf16[512,1536]{1,0:T(8,128)(2,1)}, bf16[512,1536]{1,0:T(8,128)(2,1)S(1)}, u32[]{:S(2)}, u32[]{:S(2)}) collective-permute-start(bf16[512,1536]{1,0:T(8,128)(2,1)} %get-tuple-element.134), channel_id=1, source_target_pairs={{0,1},{1,0},{2,3},{3,2},{4,5},{5,4},{6,7},{7,6},{8,9},{9,8},{10,11... | collective-permute-start | bytes 4718600 | tf_op jit(solution)/shard_map/ppermute | solution.py:754
  264.9 64.2 %collective-permute-start.12 = (bf16[8,96,2048]{2,1,0:T(8,128)(2,1)}, bf16[8,96,2048]{2,1,0:T(8,128)(2,1)}, u32[]{:S(2)}, u32[]{:S(2)}) collective-permute-start(bf16[8,96,2048]{2,1,0:T(8,128)(2,1)} %get-tuple-element.140), channel_id=1, source_target_pairs={{0,2},{2,0},{4,6},{6,4},{8,10},{10,8},{12,14},{14,12},{16,18},{18,... | collective-permute-start | bytes 9437192 | tf_op jit(solution)/shard_map/ppermute | solution.py:700
  265.0 86.5 %collective-permute-start.5 = (bf16[512,1536]{1,0:T(8,128)(2,1)}, bf16[512,1536]{1,0:T(8,128)(2,1)}, u32[]{:S(2)}, u32[]{:S(2)}) collective-permute-start(bf16[512,1536]{1,0:T(8,128)(2,1)} %get-tuple-element.111), channel_id=1, source_target_pairs={{0,1},{1,0},{2,3},{3,2},{4,5},{5,4},{6,7},{7,6},{8,9},{9,8},{10,11... | collective-permute-start | bytes 4718600 | tf_op jit(solution)/shard_map/ppermute | solution.py:754
  268.1 20.5 %collective-permute-start.26 = (bf16[1,96,2048]{2,1,0:T(8,128)(2,1)S(1)}, bf16[1,96,2048]{2,1,0:T(8,128)(2,1)S(1)}, u32[]{:S(2)}, u32[]{:S(2)}) collective-permute-start(bf16[1,96,2048]{2,1,0:T(8,128)(2,1)S(1)} %add_convert_fusion.14), channel_id=1, source_target_pairs={{0,16},{2,18},{4,20},{6,22},{8,24},{10,26},{12,28},{14,30},{16,0},... | collective-permute-start | bytes 1179656 | tf_op jit(solution)/shard_map/ppermute | solution.py:700
  293.9 33.6 %collective-permute-start.15 = (bf16[2,96,2048]{2,1,0:T(8,128)(2,1)}, bf16[2,96,2048]{2,1,0:T(8,128)(2,1)}, u32[]{:S(2)}, u32[]{:S(2)}) collective-permute-start(bf16[2,96,2048]{2,1,0:T(8,128)(2,1)} %add_convert_fusion.10), channel_id=1, source_target_pairs={{0,8},{2,10},{4,12},{6,14},{8,0},{10,2},{12,4},{14,6},{16,24},{18,... | collective-permute-start | bytes 2359304 | tf_op jit(solution)/shard_map/ppermute | solution.py:700
  293.9 32.2 %copy-start.14 = (f32[8,1536]{1,0:T(8,128)S(1)}, f32[8,1536]{1,0:T(8,128)}, u32[]{:S(2)}) copy-start(f32[8,1536]{1,0:T(8,128)} %get-tuple-element.152) | copy-start | bytes 147460
  327.0 33.1 %collective-permute-start.11 = (f32[1536]{0:T(1024)S(1)}, f32[1536]{0:T(1024)S(1)}, u32[]{:S(2)}, u32[]{:S(2)}) collective-permute-start(f32[1536]{0:T(1024)S(1)} %get-tuple-element.227), channel_id=1, source_target_pairs={{0,1},{1,0},{2,3},{3,2},{4,5},{5,4},{6,7},{7,6},{8,9},{9,8},{10,11... | collective-permute-start | bytes 18440 | tf_op jit(solution)/shard_map/ppermute | solution.py:754
  332.8 46.4 %collective-permute-start.13 = (bf16[4,96,2048]{2,1,0:T(8,128)(2,1)}, bf16[4,96,2048]{2,1,0:T(8,128)(2,1)}, u32[]{:S(2)}, u32[]{:S(2)}) collective-permute-start(bf16[4,96,2048]{2,1,0:T(8,128)(2,1)} %add_convert_fusion.1), channel_id=1, source_target_pairs={{0,4},{2,6},{4,0},{6,2},{8,12},{10,14},{12,8},{14,10},{16,20},{18,... | collective-permute-start | bytes 4718600 | tf_op jit(solution)/shard_map/ppermute | solution.py:700
  351.5 49.6 %collective-permute-start.20 = (bf16[8,96,2304]{2,1,0:T(8,128)(2,1)}, bf16[8,96,2304]{2,1,0:T(8,128)(2,1)}, u32[]{:S(2)}, u32[]{:S(2)}) collective-permute-start(bf16[8,96,2304]{2,1,0:T(8,128)(2,1)} %get-tuple-element.177), channel_id=1, source_target_pairs={{0,2},{2,0},{4,6},{6,4},{8,10},{10,8},{12,14},{14,12},{16,18},{18,... | collective-permute-start | bytes 10616840 | tf_op jit(solution)/shard_map/ppermute | solution.py:700
  355.0 5.1 copy-start.19
  355.0 5.1 copy-start.20
  355.0 21.5 %collective-permute-start.24 = (bf16[1,96,2048]{2,1,0:T(8,128)(2,1)S(1)}, bf16[1,96,2048]{2,1,0:T(8,128)(2,1)}, u32[]{:S(2)}, u32[]{:S(2)}) collective-permute-start(bf16[1,96,2048]{2,1,0:T(8,128)(2,1)S(1)} %add_convert_fusion.15), channel_id=1, source_target_pairs={{0,16},{2,18},{4,20},{6,22},{8,24},{10,26},{12,28},{14,30},{16,0},... | collective-permute-start | bytes 1179656 | tf_op jit(solution)/shard_map/ppermute | solution.py:700
  360.1 2.1 copy-start.17
  360.1 36.9 %collective-permute-start.10 = (bf16[512,1536]{1,0:T(8,128)(2,1)}, bf16[512,1536]{1,0:T(8,128)(2,1)}, u32[]{:S(2)}, u32[]{:S(2)}) collective-permute-start(bf16[512,1536]{1,0:T(8,128)(2,1)} %get-tuple-element.151), channel_id=1, source_target_pairs={{0,1},{1,0},{2,3},{3,2},{4,5},{5,4},{6,7},{7,6},{8,9},{9,8},{10,11... | collective-permute-start | bytes 4718600 | tf_op jit(solution)/shard_map/ppermute | solution.py:754
  381.2 1.1 copy-start.2
  382.3 14.7 %copy-start = (bf16[1024,1536]{1,0:T(8,128)(2,1)S(1)}, bf16[1024,1536]{1,0:T(8,128)(2,1)}, u32[]{:S(2)}) copy-start(bf16[1024,1536]{1,0:T(8,128)(2,1)} %x_ref.9) | copy-start | bytes 9437188
  382.3 14.7 %copy-start.13 = (f32[1536]{0:T(1024)S(1)}, f32[1536]{0:T(1024)}, u32[]{:S(2)}) copy-start(f32[1536]{0:T(1024)} %param.18) | copy-start | bytes 18436
  395.9 5.2 copy-start.4
  396.0 13.8 %collective-permute-start.16 = (bf16[8,96,1920]{2,1,0:T(8,128)(2,1)}, bf16[8,96,1920]{2,1,0:T(8,128)(2,1)S(1)}, u32[]{:S(2)}, u32[]{:S(2)}) collective-permute-start(bf16[8,96,1920]{2,1,0:T(8,128)(2,1)} %get-tuple-element.181), channel_id=1, source_target_pairs={{0,2},{2,0},{4,6},{6,4},{8,10},{10,8},{12,14},{14,12},{16,18},{18,... | collective-permute-start | bytes 8847368 | tf_op jit(solution)/shard_map/ppermute | solution.py:700
  397.0 6.8 %copy-start.9 = (f32[512,1536]{1,0:T(8,128)S(1)}, f32[512,1536]{1,0:T(8,128)}, u32[]{:S(2)}) copy-start(f32[512,1536]{1,0:T(8,128)} %get-tuple-element.133) | copy-start | bytes 9437188
  397.0 6.8 %copy-start.10 = (f32[512,1536]{1,0:T(8,128)S(1)}, f32[512,1536]{1,0:T(8,128)}, u32[]{:S(2)}) copy-start(f32[512,1536]{1,0:T(8,128)} %get-tuple-element.150) | copy-start | bytes 9437188
  401.1 2.8 copy-start.1
  401.1 2.8 copy-start.3
  403.2 41.6 %collective-permute-start.21 = (bf16[4,96,2304]{2,1,0:T(8,128)(2,1)S(1)}, bf16[4,96,2304]{2,1,0:T(8,128)(2,1)S(1)}, u32[]{:S(2)}, u32[]{:S(2)}) collective-permute-start(bf16[4,96,2304]{2,1,0:T(8,128)(2,1)S(1)} %add_convert_fusion), channel_id=1, source_target_pairs={{0,4},{2,6},{4,0},{6,2},{8,12},{10,14},{12,8},{14,10},{16,20},{18,... | collective-permute-start | bytes 5308424 | tf_op jit(solution)/shard_map/ppermute | solution.py:700
  407.8 19.1 %collective-permute-start.27 = (bf16[2,96,2048]{2,1,0:T(8,128)(2,1)S(1)}, bf16[2,96,2048]{2,1,0:T(8,128)(2,1)S(1)}, u32[]{:S(2)}, u32[]{:S(2)}) collective-permute-start(bf16[2,96,2048]{2,1,0:T(8,128)(2,1)S(1)} %add_convert_fusion.9), channel_id=1, source_target_pairs={{0,8},{2,10},{4,12},{6,14},{8,0},{10,2},{12,4},{14,6},{16,24},{18,... | collective-permute-start | bytes 2359304 | tf_op jit(solution)/shard_map/ppermute | solution.py:700
  407.9 3.0 copy-start.11
  411.2 63.9 %collective-permute-start.17 = (bf16[4,96,1920]{2,1,0:T(8,128)(2,1)S(1)}, bf16[4,96,1920]{2,1,0:T(8,128)(2,1)S(1)}, u32[]{:S(2)}, u32[]{:S(2)}) collective-permute-start(bf16[4,96,1920]{2,1,0:T(8,128)(2,1)S(1)} %add_convert_fusion.6), channel_id=1, source_target_pairs={{0,4},{2,6},{4,0},{6,2},{8,12},{10,14},{12,8},{14,10},{16,20},{18,... | collective-permute-start | bytes 4423688 | tf_op jit(solution)/shard_map/ppermute | solution.py:700
  428.4 19.2 %collective-permute-start.28 = (bf16[1,96,2048]{2,1,0:T(8,128)(2,1)S(1)}, bf16[1,96,2048]{2,1,0:T(8,128)(2,1)S(1)}, u32[]{:S(2)}, u32[]{:S(2)}) collective-permute-start(bf16[1,96,2048]{2,1,0:T(8,128)(2,1)S(1)} %add_convert_fusion.13), channel_id=1, source_target_pairs={{0,16},{2,18},{4,20},{6,22},{8,24},{10,26},{12,28},{14,30},{16,0},... | collective-permute-start | bytes 1179656 | tf_op jit(solution)/shard_map/ppermute | solution.py:700
  446.3 29.2 %collective-permute-start.22 = (bf16[2,96,2304]{2,1,0:T(8,128)(2,1)S(1)}, bf16[2,96,2304]{2,1,0:T(8,128)(2,1)S(1)}, u32[]{:S(2)}, u32[]{:S(2)}) collective-permute-start(bf16[2,96,2304]{2,1,0:T(8,128)(2,1)S(1)} %add_convert_fusion.7), channel_id=1, source_target_pairs={{0,8},{2,10},{4,12},{6,14},{8,0},{10,2},{12,4},{14,6},{16,24},{18,... | collective-permute-start | bytes 2654216 | tf_op jit(solution)/shard_map/ppermute | solution.py:700
  475.4 26.8 %collective-permute-start.18 = (bf16[2,96,1920]{2,1,0:T(8,128)(2,1)S(1)}, bf16[2,96,1920]{2,1,0:T(8,128)(2,1)S(1)}, u32[]{:S(2)}, u32[]{:S(2)}) collective-permute-start(bf16[2,96,1920]{2,1,0:T(8,128)(2,1)S(1)} %add_convert_fusion.11), channel_id=1, source_target_pairs={{0,8},{2,10},{4,12},{6,14},{8,0},{10,2},{12,4},{14,6},{16,24},{18,... | collective-permute-start | bytes 2211848 | tf_op jit(solution)/shard_map/ppermute | solution.py:700
  476.8 26.1 %collective-permute-start.23 = (bf16[1,96,2304]{2,1,0:T(8,128)(2,1)S(1)}, bf16[1,96,2304]{2,1,0:T(8,128)(2,1)S(1)}, u32[]{:S(2)}, u32[]{:S(2)}) collective-permute-start(bf16[1,96,2304]{2,1,0:T(8,128)(2,1)S(1)} %add_convert_fusion.12), channel_id=1, source_target_pairs={{0,16},{2,18},{4,20},{6,22},{8,24},{10,26},{12,28},{14,30},{16,0},... | collective-permute-start | bytes 1327112 | tf_op jit(solution)/shard_map/ppermute | solution.py:700
  502.4 17.3 %collective-permute-start.19 = (bf16[1,96,1920]{2,1,0:T(8,128)(2,1)S(1)}, bf16[1,96,1920]{2,1,0:T(8,128)(2,1)S(1)}, u32[]{:S(2)}, u32[]{:S(2)}) collective-permute-start(bf16[1,96,1920]{2,1,0:T(8,128)(2,1)S(1)} %add_convert_fusion.16), channel_id=1, source_target_pairs={{0,16},{2,18},{4,20},{6,22},{8,24},{10,26},{12,28},{14,30},{16,0},... | collective-permute-start | bytes 1105928 | tf_op jit(solution)/shard_map/ppermute | solution.py:700
